TPU v7x, 32 devices: a whole 2x2x4 slice. The times are simulated.
32 devices in a mesh: tx: 8 (over y, x, core), ty: 4 (over z).
Axes of the slice: x: 2, y: 2, z: 4, core: 2. Of those that a mesh axis runs over, the one named last changes fastest.
Arguments:
- pressure: float32 [128, 64, 1], P('tx', 'ty'), may hold values from -6 to 6
- mobility: float32 [11, 128, 64, 1], P(None, 'tx', 'ty'), may hold values from 0.05 to 1
- mob_deriv: float32 [121, 128, 64, 1], P(None, 'tx', 'ty'), may hold values from -6 to 6
- accum: float32 [121, 128, 64, 1], P(None, 'tx', 'ty'), may hold values from -6 to 6
- trans: float32 [3, 128, 64, 1], P(None, 'tx', 'ty'), may hold values from 0.1 to 2
- upwind: int32 [3, 128, 64, 1], P(None, 'tx', 'ty'), may hold values 0 or 1
- fault_send: int32 [32, 32, 2], P(('tx', 'ty')), may hold values from 0 to 255
- fault_cell: int32 [32, 64], P(('tx', 'ty')), may hold values from 0 to 255, as said below
- fault_slot: int32 [32, 64], P(('tx', 'ty')), may hold values from 0 to 63, each once within a row
- fault_trans: float32 [32, 64], P(('tx', 'ty')), may hold values from 0.1 to 2
- fault_up: int32 [32, 64], P(('tx', 'ty')), may hold values 0 or 1
- cell_owner: int32 [8192, 1], P(('tx', 'ty')), may hold values from 0 to 31; in each aligned block of 256 rows (0 to 255, 256 to 511, ...) at most 16 rows name the same one
Outputs:
- relaid: bfloat16 [16384, 8, 256], P(('tx', 'ty'))
Inputs may be any that keep to these rules, and one draw needn't show every extreme that they name: `fault_cell`: each tile's 64 entries are distinct local cells. `fault_slot`: each tile's row is a permutation of the received slots. `fault_send`: local cell indices of the sending tile. `cell_owner`: among the cells of one tile (aligned blocks of 256 in global cell order) at most 16 have the same owner.
All inputs are finite; a program needn't handle non-finite values. No bound on the sum of `upwind` or of `fault_up` on one device may be relied on, other than what follows from the above.
Results may differ from a plain program's by a relative error of at most 0.0045.
Values may be sent and summed in bfloat16 or wider, within the bound.
A program may use at most 64 MiB of HBM per device.

v0:
```python
import jax
import jax.numpy as jnp
from jax import lax
from jax.sharding import PartitionSpec as P

PAD = 16


def with_halo(cells, sides, width):
    for axis, dim in sides:
        count = lax.axis_size(axis)
        ends = count - 1
        head = lax.slice_in_dim(cells, 0, width, axis=dim)
        tail = lax.slice_in_dim(cells, cells.shape[dim] - width, cells.shape[dim], axis=dim)
        cells = jnp.concatenate(
            [
                lax.ppermute(tail, axis, [(i, (i + 1) % count) for i in range(ends)]),
                cells,
                lax.ppermute(head, axis, [((i + 1) % count, i) for i in range(ends)]),
            ],
            axis=dim,
        )
    return cells


def direction_terms(state_self, state_other, conduct, self_up, count):
    rest = state_self.shape[1:]
    lower = 1.0 - self_up
    diff = state_self[0] - state_other[0]
    mob_up = self_up * state_self[1 : count + 1] + lower * state_other[1 : count + 1]
    deriv_self = state_self[count + 1 :].reshape((count, count) + rest)
    deriv_other = state_other[count + 1 :].reshape((count, count) + rest)
    column = (jnp.arange(count) == 0).astype(jnp.float32).reshape((1, count) + (1,) * len(rest))
    pressure_part = mob_up[:, None] * column
    diag_part = conduct * (self_up * diff * deriv_self + pressure_part)
    off_part = conduct * (lower * diff * deriv_other - pressure_part)
    return (diag_part, off_part)


def shift_down(field):
    zero_plane = jnp.zeros(field.shape[:-1] + (1,), field.dtype)
    return jnp.concatenate([zero_plane, field[..., :-1]], -1)


def shift_up(field):
    zero_plane = jnp.zeros(field.shape[:-1] + (1,), field.dtype)
    return jnp.concatenate([field[..., 1:], zero_plane], -1)


def body(
    pressure,
    mobility,
    mob_deriv,
    accum,
    trans,
    upwind,
    fault_send,
    fault_cell,
    fault_slot,
    fault_trans,
    fault_up,
    cell_owner,
):
    width_x, width_y, depth = pressure.shape
    count = mobility.shape[0]
    cells = width_x * width_y * depth
    span_x = lax.axis_size("tx")
    span_y = lax.axis_size("ty")
    devices = span_x * span_y
    capacity = max(2, 2 * cells // devices)
    state = jnp.concatenate([pressure[None], mobility, mob_deriv], 0)
    nstate = state.shape[0]
    flat_state = state.reshape(nstate, cells)
    picks = fault_send[0].reshape(-1)
    outgoing = jnp.take(flat_state, picks, axis=1).reshape(nstate, devices, -1)
    arrived = lax.all_to_all(
        outgoing.astype(jnp.bfloat16), ("tx", "ty"), split_axis=1, concat_axis=1, tiled=True
    ).astype(outgoing.dtype)
    arrived = arrived.reshape(nstate, -1)
    flags = upwind.astype(jnp.float32)
    carried = jnp.concatenate([state, trans[0:2], flags[0:2]], 0)
    padded = with_halo(carried, (("tx", 1), ("ty", 2)), 1)
    lower_x = padded[:, 0:width_x, 1 : width_y + 1]
    upper_x = padded[:, 2 : width_x + 2, 1 : width_y + 1]
    lower_y = padded[:, 1 : width_x + 1, 0:width_y]
    upper_y = padded[:, 1 : width_x + 1, 2 : width_y + 2]
    pos_x = lax.axis_index("tx") * width_x + jnp.arange(width_x)
    pos_y = lax.axis_index("ty") * width_y + jnp.arange(width_y)
    keep_x = (pos_x < span_x * width_x - 1).astype(jnp.float32)[:, None, None]
    keep_y = (pos_y < span_y * width_y - 1).astype(jnp.float32)[None, :, None]
    keep_z = (jnp.arange(depth) < depth - 1).astype(jnp.float32)[None, None, :]
    pairs = [
        (lower_x[:nstate], lower_x[nstate], 1.0 - lower_x[nstate + 2]),
        (upper_x[:nstate], trans[0] * keep_x, flags[0]),
        (lower_y[:nstate], lower_y[nstate + 1], 1.0 - lower_y[nstate + 3]),
        (upper_y[:nstate], trans[1] * keep_y, flags[1]),
        (shift_down(state), shift_down(trans[2]), 1.0 - shift_down(flags[2])),
        (shift_up(state), trans[2] * keep_z, flags[2]),
    ]
    diag = accum.reshape((count, count, width_x, width_y, depth))
    offs = []
    for other, conduct, self_up in pairs:
        diag_part, off_part = direction_terms(state, other, conduct, self_up, count)
        diag = diag + diag_part
        offs.append(off_part.reshape(count, count, cells))
    own_cells = fault_cell[0]
    partner = jnp.take(arrived, fault_slot[0], axis=1)
    mine = jnp.take(flat_state, own_cells, axis=1)
    fault_diag, fault_off = direction_terms(
        mine, partner, fault_trans[0], fault_up[0].astype(jnp.float32), count
    )
    fault_table = (own_cells[:, None] == jnp.arange(cells, dtype=jnp.int32)[None, :]).astype(
        jnp.float32
    )
    fault_pair = jnp.concatenate(
        [fault_diag.reshape(count * count, -1), fault_off.reshape(count * count, -1)], 0
    )
    placed = jnp.dot(
        fault_pair, fault_table, precision=lax.Precision.HIGHEST, preferred_element_type=jnp.float32
    )
    diag_flat = diag.reshape(count, count, cells) + placed[: count * count].reshape(
        count, count, cells
    )
    fault_block = placed[count * count :].reshape(count, count, cells)
    stacked = jnp.stack([diag_flat] + offs + [fault_block], 0).astype(jnp.bfloat16)
    full = jnp.pad(stacked, ((0, 0), (0, PAD - count), (0, PAD - count), (0, 0)))
    flat_rows = full.reshape(8 * PAD * PAD, cells)
    owner = cell_owner[:, 0]
    onehot = (owner[:, None] == jnp.arange(devices, dtype=jnp.int32)[None, :]).astype(jnp.bfloat16)
    before = (jnp.arange(cells)[None, :] < jnp.arange(cells)[:, None]).astype(jnp.bfloat16)
    earlier = jnp.dot(before, onehot, preferred_element_type=jnp.float32)
    rank = jnp.sum(earlier * onehot.astype(jnp.float32), 1).astype(jnp.int32)
    slot = owner * capacity + rank
    placement = (jnp.arange(devices * capacity, dtype=jnp.int32)[:, None] == slot[None, :]).astype(
        jnp.bfloat16
    )
    buffer = lax.dot_general(
        placement, flat_rows, (((1,), (1,)), ((), ())), preferred_element_type=jnp.float32
    ).astype(jnp.bfloat16)
    landed = lax.all_to_all(
        buffer.reshape(devices, capacity, -1), ("tx", "ty"), split_axis=0, concat_axis=0, tiled=True
    )
    landed = landed.reshape(devices * capacity, -1)
    return landed.reshape(-1, 8, PAD * PAD)


def solution(mesh):
    in_specs = (
        P("tx", "ty", None),
        P(None, "tx", "ty", None),
        P(None, "tx", "ty", None),
        P(None, "tx", "ty", None),
        P(None, "tx", "ty", None),
        P(None, "tx", "ty", None),
        P(("tx", "ty"), None, None),
        P(("tx", "ty"), None),
        P(("tx", "ty"), None),
        P(("tx", "ty"), None),
        P(("tx", "ty"), None),
        P(("tx", "ty"), None),
    )
    out_specs = P(("tx", "ty"), None, None)
    return jax.shard_map(body, mesh=mesh, in_specs=in_specs, out_specs=out_specs, check_vma=False)
```

profile of v0, /device:TPU:0, one launch (start us, length us, event | category | flops | bytes accessed | tf_op | source)
XLA Modules:
  0.0 135.7 jit_solution(10856896059263928000)
XLA Ops:
  0.0 0.8 convert_element_type.93
  1.0 1.1 copy.254
  3.0 0.9 copy.253
  3.8 1.1 concatenate.31
  5.0 2.4 %collective-permute-start = (f32[137,1,16,1]{0,2,3,1:T(8,128)S(1)}, f32[137,1,16,1]{0,2,3,1:T(8,128)S(1)}, u32[]{:S(2)}, u32[]{:S(2)}) collective-permute-start(f32[137,1,16,1]{0,2,3,1:T(8,128)S(1)} %get-tuple-element.29), channel_id=1, source_target_pairs={{0,4},{4,8},{8,12},{12,16},{16,20},{20,24},{24,28},{1,5},{5,9},{9,... | collective-permute-start | bytes 26312 | tf_op jit(solution)/shard_map/ppermute | solution.py:17
  7.4 1.3 collective-permute-start.1
  10.8 9.3 %all-to-all-start = ((bf16[133,32,2]{0,2,1:T(2,128)(2,1)}), bf16[133,32,2]{0,2,1:T(2,128)(2,1)}, u32[]{:S(2)}, u32[]{:S(2)}) async-start(bf16[133,32,2]{0,2,1:T(2,128)(2,1)} %convert_element_type.100), calls=%async_computation | async-start | bytes 65536 | tf_op jit(solution)/shard_map/all_to_all | solution.py:76
  29.0 1.0 reshape.778
  30.0 1.0 reshape.779
  34.6 4.2 %collective-permute-start.2 = (f32[137,18,1,1]{0,3,2,1:T(1,128)S(1)}, f32[137,18,1,1]{0,3,2,1:T(1,128)}, u32[]{:S(2)}, u32[]{:S(2)}) collective-permute-start(f32[137,18,1,1]{0,3,2,1:T(1,128)S(1)} %get-tuple-element.21), channel_id=1, source_target_pairs={{0,1},{1,2},{2,3},{4,5},{5,6},{6,7},{8,9},{9,10},{10,11},{12,13},{... | collective-permute-start | bytes 29600 | tf_op jit(solution)/shard_map/ppermute | solution.py:17
  38.8 1.5 %collective-permute-start.3 = (f32[137,18,1,1]{0,3,2,1:T(1,128)}, f32[137,18,1,1]{0,3,2,1:T(1,128)}, u32[]{:S(2)}, u32[]{:S(2)}) collective-permute-start(f32[137,18,1,1]{0,3,2,1:T(1,128)} %get-tuple-element.22), channel_id=1, source_target_pairs={{1,0},{2,1},{3,2},{5,4},{6,5},{7,6},{9,8},{10,9},{11,10},{13,12},{... | collective-permute-start | bytes 29600 | tf_op jit(solution)/shard_map/ppermute | solution.py:19
  41.7 1.0 copy.270
  46.7 1.0 reshape.783
  48.2 1.0 reshape.784
  49.2 1.7 %copy.269 = f32[137,18,1,1]{2,1,3,0:T(8,128)S(1)} copy(f32[137,18,1,1]{0,3,2,1:T(1,128)} %collective-permute-done.2) | data formatting | bytes 19728 | tf_op jit(solution)/shard_map/ppermute | solution.py:17
  51.7 2.8 %copy.275 = f32[137,18,1,1]{2,1,3,0:T(8,128)} copy(f32[137,18,1,1]{0,3,2,1:T(1,128)} %collective-permute-done.3) | data formatting | bytes 19728 | tf_op jit(solution)/shard_map/ppermute | solution.py:19
  54.5 3.7 %pad_maximum_fusion = (f32[121,16,16,1]{2,1,3,0:T(8,128)}, f32[121,16,16,1]{2,1,3,0:T(8,128)}) fusion(f32[137,18,1,1]{2,1,3,0:T(8,128)} %copy.275, f32[137,18,16,1]{2,1,3,0:T(8,128)S(1)} %copy.270, f32[137,18,1,1]{2,1,3,0:T(8,128)S(1)} %copy.269), kind=kLoop, calls=%fused_computation.6 | loop fusion | flops 61952 | bytes 425360 | tf_op jit(solution)/shard_map/concatenate | solution.py:15
  59.0 0.8 fusion.42
  59.9 1.1 mul.944
  61.8 1.6 %reshape.785 = f32[1,11,11,256]{3,0,2,1:T(1,128)S(1)} reshape(f32[121,16,16,1]{2,1,3,0:T(8,128)} %get-tuple-element.18) | data formatting | bytes 247808 | tf_op jit(solution)/shard_map/reshape | solution.py:32
  63.4 0.8 mul.932
  64.2 1.0 mul.963
  66.0 0.8 mul.1018
  66.7 0.8 mul.1028
  67.5 0.8 mul.1034
  68.3 0.8 mul.1039
  69.9 0.9 fusion.20
  71.2 0.8 reshape.790
  73.8 1.1 add_convert_fusion
  75.0 3.5 %stack.5 = bf16[8,11,11,256]{3,0,2,1:T(8,128)(2,1)S(1)} concatenate(bf16[1,11,11,256]{3,0,2,1:T(2,128)(2,1)S(1)} %add_convert_fusion, bf16[1,11,11,256]{3,0,2,1:T(2,128)(2,1)S(1)} %get-tuple-element.58, bf16[1,11,11,256]{3,0,2,1:T(2,128)(2,1)S(1)} %get-tuple-element.60, bf16[1,11,11,256]{3,0,2,1:T(2,128)(2,1)S(1)} %fusion.33, bf16[1,11,11,256]{3,0,2,1:T(2,128)(2,1)S(1)} %get-tuple-element.59, ...), dimensions={0} | concatenate | bytes 991232 | tf_op jit(solution)/shard_map/stack | solution.py:125
  79.8 53.9 %all_to_all.10 = bf16[32,16,2048]{2,1,0:T(8,128)(2,1)S(1)} all-to-all(bf16[32,16,2048]{2,1,0:T(8,128)(2,1)S(1)} %bitcast.195), channel_id=1, replica_groups=mesh['tx'=8,'ty'=4] {'tx','ty'}, dimensions={0} | all-to-all | bytes 4194304 | tf_op jit(solution)/shard_map/all_to_all | solution.py:140
  133.7 2.0 %copy.299 = bf16[64,8,8,256]{3,2,1,0:T(8,128)(2,1)} copy(bf16[64,8,8,256]{3,1,2,0:T(8,128)(2,1)S(1)} %bitcast.196) | data formatting | bytes 4194304
  (199 shorter events, 28.4 us)
Async XLA Ops:
  0.0 8.7 %copy-start.2 = (f32[11,16,16,1]{2,3,1,0:T(1,128)S(1)}, f32[11,16,16,1]{2,3,1,0:T(1,128)}, u32[]{:S(2)}) copy-start(f32[11,16,16,1]{2,3,1,0:T(1,128)} %param.15) | copy-start | bytes 33796
  0.0 9.1 %copy-start.14 = (f32[16,16,1]{1,2,0:T(1,128)S(1)}, f32[16,16,1]{1,2,0:T(1,128)}, u32[]{:S(2)}) copy-start(f32[16,16,1]{1,2,0:T(1,128)} %param.14) | copy-start | bytes 3076
  0.0 9.2 %copy-start.3 = (f32[121,16,16,1]{0,3,2,1:T(1,128)S(1)}, f32[121,16,16,1]{0,3,2,1:T(1,128)}, u32[]{:S(2)}) copy-start(f32[121,16,16,1]{0,3,2,1:T(1,128)} %param.16) | copy-start | bytes 371716
  0.0 8.8 %copy-start.37 = (s32[1,32,2]{1,2,0:T(2,128)S(1)}, s32[1,32,2]{1,2,0:T(2,128)}, u32[]{:S(2)}) copy-start(s32[1,32,2]{1,2,0:T(2,128)} %param.20) | copy-start | bytes 772
  0.8 20.0 %copy-start.19 = (f32[3,16,16,1]{2,3,1,0:T(1,128)S(1)}, f32[3,16,16,1]{2,3,1,0:T(1,128)}, u32[]{:S(2)}) copy-start(f32[3,16,16,1]{2,3,1,0:T(1,128)} %param.18) | copy-start | bytes 9220
  0.8 20.0 %copy-start.40 = (s32[1,64]{1,0:T(1,128)S(1)}, s32[1,64]{1,0:T(1,128)}, u32[]{:S(2)}) copy-start(s32[1,64]{1,0:T(1,128)} %param.21) | copy-start | bytes 772
  0.8 20.6 %copy-start.48 = (s32[1,64]{1,0:T(1,128)S(1)}, s32[1,64]{1,0:T(1,128)}, u32[]{:S(2)}) copy-start(s32[1,64]{1,0:T(1,128)} %param.22) | copy-start | bytes 772
  0.8 21.1 %copy-start.44 = (s32[1,64]{1,0:T(1,128)S(1)}, s32[1,64]{1,0:T(1,128)}, u32[]{:S(2)}) copy-start(s32[1,64]{1,0:T(1,128)} %param.24) | copy-start | bytes 772
  0.8 22.8 %copy-start.38 = (s32[256,1]{0,1:T(1,128)S(1)}, s32[256,1]{0,1:T(1,128)}, u32[]{:S(2)}) copy-start(s32[256,1]{0,1:T(1,128)} %param.25) | copy-start | bytes 3076
  5.0 29.0 %collective-permute-start = (f32[137,1,16,1]{0,2,3,1:T(8,128)S(1)}, f32[137,1,16,1]{0,2,3,1:T(8,128)S(1)}, u32[]{:S(2)}, u32[]{:S(2)}) collective-permute-start(f32[137,1,16,1]{0,2,3,1:T(8,128)S(1)} %get-tuple-element.29), channel_id=1, source_target_pairs={{0,4},{4,8},{8,12},{12,16},{16,20},{20,24},{24,28},{1,5},{5,9},{9,... | collective-permute-start | bytes 26312 | tf_op jit(solution)/shard_map/ppermute | solution.py:17
  7.4 26.6 %collective-permute-start.1 = (f32[137,1,16,1]{0,2,3,1:T(8,128)S(1)}, f32[137,1,16,1]{0,2,3,1:T(8,128)S(1)}, u32[]{:S(2)}, u32[]{:S(2)}) collective-permute-start(f32[137,1,16,1]{0,2,3,1:T(8,128)S(1)} %get-tuple-element.30), channel_id=1, source_target_pairs={{4,0},{8,4},{12,8},{16,12},{20,16},{24,20},{28,24},{5,1},{9,5},{13... | collective-permute-start | bytes 26312 | tf_op jit(solution)/shard_map/ppermute | solution.py:19
  9.4 19.0 %copy-start.16 = (f32[121,16,16,1]{0,3,2,1:T(1,128)S(1)}, f32[121,16,16,1]{0,3,2,1:T(1,128)}, u32[]{:S(2)}) copy-start(f32[121,16,16,1]{0,3,2,1:T(1,128)} %param.17) | copy-start | bytes 371716
  10.8 60.4 %all-to-all-start = ((bf16[133,32,2]{0,2,1:T(2,128)(2,1)}), bf16[133,32,2]{0,2,1:T(2,128)(2,1)}, u32[]{:S(2)}, u32[]{:S(2)}) async-start(bf16[133,32,2]{0,2,1:T(2,128)(2,1)} %convert_element_type.100), calls=%async_computation | async-start | bytes 65536 | tf_op jit(solution)/shard_map/all_to_all | solution.py:76
  34.6 14.6 %collective-permute-start.2 = (f32[137,18,1,1]{0,3,2,1:T(1,128)S(1)}, f32[137,18,1,1]{0,3,2,1:T(1,128)}, u32[]{:S(2)}, u32[]{:S(2)}) collective-permute-start(f32[137,18,1,1]{0,3,2,1:T(1,128)S(1)} %get-tuple-element.21), channel_id=1, source_target_pairs={{0,1},{1,2},{2,3},{4,5},{5,6},{6,7},{8,9},{9,10},{10,11},{12,13},{... | collective-permute-start | bytes 29600 | tf_op jit(solution)/shard_map/ppermute | solution.py:17
  38.8 12.8 %collective-permute-start.3 = (f32[137,18,1,1]{0,3,2,1:T(1,128)}, f32[137,18,1,1]{0,3,2,1:T(1,128)}, u32[]{:S(2)}, u32[]{:S(2)}) collective-permute-start(f32[137,18,1,1]{0,3,2,1:T(1,128)} %get-tuple-element.22), channel_id=1, source_target_pairs={{1,0},{2,1},{3,2},{5,4},{6,5},{7,6},{9,8},{10,9},{11,10},{13,12},{... | collective-permute-start | bytes 29600 | tf_op jit(solution)/shard_map/ppermute | solution.py:19
  59.8 9.3 %copy-start.1 = (f32[121,16,16,1]{2,1,3,0:T(8,128)S(1)}, f32[121,16,16,1]{2,1,3,0:T(8,128)}, u32[]{:S(2)}) copy-start(f32[121,16,16,1]{2,1,3,0:T(8,128)} %get-tuple-element.17) | copy-start | bytes 371716
  59.8 9.7 %copy-start.33 = (f32[11]{0:T(128)S(1)}, f32[11]{0:T(128)}, u32[]{:S(2)}) copy-start(f32[11]{0:T(128)} %copy-done.32) | copy-start | bytes 136
  59.8 10.0 %copy-start.6 = (f32[1,11,11,256]{3,0,2,1:T(1,128)S(1)}, f32[1,11,11,256]{3,0,2,1:T(1,128)}, u32[]{:S(2)}) copy-start(f32[1,11,11,256]{3,0,2,1:T(1,128)} %reshape.783) | copy-start | bytes 371716
  59.8 10.0 %copy-start.7 = (f32[1,11,11,256]{3,0,2,1:T(1,128)S(1)}, f32[1,11,11,256]{3,0,2,1:T(1,128)}, u32[]{:S(2)}) copy-start(f32[1,11,11,256]{3,0,2,1:T(1,128)} %reshape.784) | copy-start | bytes 371716
  59.8 10.0 %copy-start.8 = (f32[11,256]{1,0:T(8,128)S(1)}, f32[11,256]{1,0:T(8,128)}, u32[]{:S(2)}) copy-start(f32[11,256]{1,0:T(8,128)} %copy.279) | copy-start | bytes 33796
  59.8 10.0 %copy-start.9 = (f32[11,256]{1,0:T(8,128)S(1)}, f32[11,256]{1,0:T(8,128)}, u32[]{:S(2)}) copy-start(f32[11,256]{1,0:T(8,128)} %copy.263) | copy-start | bytes 33796
  59.8 10.0 %copy-start.10 = (f32[11,256]{1,0:T(8,128)S(1)}, f32[11,256]{1,0:T(8,128)}, u32[]{:S(2)}) copy-start(f32[11,256]{1,0:T(8,128)} %copy.267) | copy-start | bytes 33796
  59.8 10.0 %copy-start.11 = (f32[11,256]{1,0:T(8,128)S(1)}, f32[11,256]{1,0:T(8,128)}, u32[]{:S(2)}) copy-start(f32[11,256]{1,0:T(8,128)} %mul.987) | copy-start | bytes 33796
  59.9 10.0 %copy-start.29 = (f32[256]{0:T(256)S(1)}, f32[256]{0:T(256)}, u32[]{:S(2)}) copy-start(f32[256]{0:T(256)} %mul.916) | copy-start | bytes 3076
  59.9 10.0 %copy-start.30 = (f32[256]{0:T(256)S(1)}, f32[256]{0:T(256)}, u32[]{:S(2)}) copy-start(f32[256]{0:T(256)} %mul.951) | copy-start | bytes 3076
  59.9 10.0 %copy-start.31 = (f32[256]{0:T(256)S(1)}, f32[256]{0:T(256)}, u32[]{:S(2)}) copy-start(f32[256]{0:T(256)} %mul.896) | copy-start | bytes 3076
  61.7 9.0 %copy-start.13 = (f32[1,16,16,1]{2,1,3,0:T(8,128)S(1)}, f32[1,16,16,1]{2,1,3,0:T(8,128)}, u32[]{:S(2)}) copy-start(f32[1,16,16,1]{2,1,3,0:T(8,128)} %copy-done.12) | copy-start | bytes 3076
  61.7 9.0 %copy-start.27 = (f32[16,16,1]{1,0,2:T(8,128)S(1)}, f32[16,16,1]{1,0,2:T(8,128)}, u32[]{:S(2)}) copy-start(f32[16,16,1]{1,0,2:T(8,128)} %get-tuple-element.38) | copy-start | bytes 3076
  61.7 9.0 %copy-start.28 = (f32[16,16,1]{1,0,2:T(8,128)S(1)}, f32[16,16,1]{1,0,2:T(8,128)}, u32[]{:S(2)}) copy-start(f32[16,16,1]{1,0,2:T(8,128)} %get-tuple-element.40) | copy-start | bytes 3076
  61.7 9.2 %copy-start.26 = (f32[16,16,1]{1,0,2:T(8,128)S(1)}, f32[16,16,1]{1,0,2:T(8,128)}, u32[]{:S(2)}) copy-start(f32[16,16,1]{1,0,2:T(8,128)} %get-tuple-element.53) | copy-start | bytes 3076
  61.8 9.3 %copy-start.25 = (f32[16,16,1]{1,0,2:T(8,128)S(1)}, f32[16,16,1]{1,0,2:T(8,128)}, u32[]{:S(2)}) copy-start(f32[16,16,1]{1,0,2:T(8,128)} %get-tuple-element.36) | copy-start | bytes 3076
  61.8 9.4 %copy-start.24 = (f32[16,16,1]{1,0,2:T(8,128)S(1)}, f32[16,16,1]{1,0,2:T(8,128)}, u32[]{:S(2)}) copy-start(f32[16,16,1]{1,0,2:T(8,128)} %get-tuple-element.43) | copy-start | bytes 3076
  (22 other events, 69.3 us)
where the time goes:
time: 138 us; the launch traced here: 136 us
  blocking collectives  53.9 us (39%)
  local copies, waits for them, and re-layouts  45 us (33%)
  starting transfers between devices  18.6 us (13%)
  other arithmetic  16 us (12%)
    all_to_all x1, blocking collectives, body(): lax.all_to_all(buffer.reshape(devices, capacity, -1), ('tx', 'ty'), split...  53.9 us
    all_to_all x1, starting transfers between devices, body(): lax.all_to_all(outgoing.astype(jnp.bfloat16), ('tx', 'ty'), split_axis=1,...  9.34 us
    unnamed x110, local copies, waits for them, and re-layouts  8.44 us
    ppermute x2, starting transfers between devices, with_halo(): lax.ppermute(tail, axis, [(i, (i + 1) % count) for i in range(ends)])  6.56 us
    mul x10, local copies, waits for them, and re-layouts, direction_terms(): pressure_part = mob_up[:, None] * column  5.46 us
    mul x6, local copies, waits for them, and re-layouts, direction_terms(): off_part = conduct * (lower * diff * deriv_other - pressure_part)  4.66 us
    reshape x4, local copies, waits for them, and re-layouts, direction_terms(): deriv_other = state_other[count + 1:].reshape((count, count) + rest)  4.07 us
    concatenate x3, other arithmetic, with_halo(): jnp.concatenate([lax.ppermute(tail, axis, [(i, (i + 1) % count) for i in...  3.82 us
  transfers between devices with their start and end apart: 5, of which 0 were waited for; matrix products, arithmetic and copies ran while one was open for 34% of the time, Pallas kernels for 0%

commit v1 on v0

v1 whole, which is shorter than its diff:
```python
import functools

import jax
import jax.numpy as jnp
from jax import lax
from jax.experimental import pallas as pl
from jax.experimental.pallas import tpu as pltpu
from jax.sharding import PartitionSpec as P

PAD = 16
BLOCKS = 8
LANES = 128
ROWS = 16
MESH = pl.DeviceIdType.MESH
EXACT = lax.Precision.HIGHEST
F32 = jnp.float32
BF16 = jnp.bfloat16
NT = (((1,), (1,)), ((), ()))
TN = (((0,), (0,)), ((), ()))
VMEM_LIMIT = 48 * 1024 * 1024


def iota(shape, dim):
    return lax.broadcasted_iota(jnp.int32, shape, dim)


def build_kernel(
    span_x,
    span_y,
    width,
    count,
    p_ref,
    m_ref,
    deriv_ref,
    acc_ref,
    trans_ref,
    up_ref,
    fsend_ref,
    fcell_ref,
    fslot_ref,
    ftrans_ref,
    fup_ref,
    owner_ref,
    land_off,
    land_diag,
    state_l,
    state_m,
    lower_y_l,
    lower_y_m,
    upper_y_l,
    upper_y_m,
    halo_out,
    halo_in,
    fault_out,
    fault_in,
    send_off,
    send_diag,
    halo_ssem,
    halo_rsem,
    fault_ssem,
    fault_rsem,
    off_ssem,
    off_rsem,
    diag_ssem,
    diag_rsem,
    own_sem,
):
    devices = span_x * span_y
    cells = width * width
    entries = count * count
    shift = width.bit_length() - 1
    lane_p, lane_t, lane_w = entries, entries + 1, entries + 3
    tx = lax.axis_index("tx")
    ty = lax.axis_index("ty")
    me = tx * span_y + ty

    def place(device):
        return (lax.div(device, span_y), lax.rem(device, span_y))

    def partner(step):
        return lax.rem(me + step, devices)

    barrier = pltpu.get_barrier_semaphore()

    def greet(step, carry):
        pl.semaphore_signal(
            barrier, inc=1, device_id=place(partner(step)), device_id_type=MESH
        )
        return carry

    lax.fori_loop(1, devices, greet, 0)

    fields = jnp.concatenate(
        [
            p_ref[...],
            m_ref[...],
            trans_ref[0 : 2 * width, :],
            up_ref[0 : 2 * width, :].astype(F32),
        ],
        0,
    )
    nfield = fields.shape[0]
    spread = ((iota((cells, width), 0) & (width - 1)) == iota((cells, width), 1)).astype(F32)
    crossed = lax.dot_general(spread, fields, NT, precision=EXACT, preferred_element_type=F32)
    same = (iota((cells, nfield), 1) & (width - 1)) == (iota((cells, nfield), 0) >> shift)
    kind = iota((nfield, LANES), 0) >> shift
    lane_of = jnp.where(
        kind == 0,
        lane_p,
        jnp.where(kind <= count, (kind - 1) * count, kind - (count + 1) + lane_t),
    )
    sorter = (iota((nfield, LANES), 1) == lane_of).astype(F32)
    misc = jnp.dot(
        jnp.where(same, crossed, 0.0), sorter, precision=EXACT, preferred_element_type=F32
    )
    state_m[...] = misc
    state_l[...] = jnp.zeros_like(state_l)
    state_l[:, 0:entries] = deriv_ref[...]
    deriv = state_l[...]

    last = cells - width
    halo_out[0, 0:width] = deriv[0:width]
    halo_out[0, width : 2 * width] = misc[0:width]
    halo_out[1, 0:width] = deriv[last:]
    halo_out[1, width : 2 * width] = misc[last:]
    for side, start in ((2, 0), (3, width - 1)):
        halo_out[side, 0:width] = state_l[pl.ds(start, width, stride=width), :]
        halo_out[side, width : 2 * width] = state_m[pl.ds(start, width, stride=width), :]

    ends = (tx > 0, tx < span_x - 1, ty > 0, ty < span_y - 1)
    targets = ((tx - 1, ty), (tx + 1, ty), (tx, ty - 1), (tx, ty + 1))

    def halo_copy(side):
        return pltpu.make_async_remote_copy(
            src_ref=halo_out.at[side],
            dst_ref=halo_in.at[side ^ 1],
            send_sem=halo_ssem.at[side],
            recv_sem=halo_rsem.at[side ^ 1],
            device_id=targets[side],
            device_id_type=MESH,
        )

    def block_copy(src, dst, ssem, rsem, step):
        device = partner(step)
        return pltpu.make_async_remote_copy(
            src_ref=src.at[device],
            dst_ref=dst.at[me],
            send_sem=ssem.at[device],
            recv_sem=rsem.at[me],
            device_id=place(device),
            device_id_type=MESH,
        )

    def block_arrival(src, dst, ssem, rsem, step):
        device = partner(step)
        return pltpu.make_async_remote_copy(
            src_ref=src.at[device],
            dst_ref=dst.at[device],
            send_sem=ssem.at[device],
            recv_sem=rsem.at[device],
            device_id=place(device),
            device_id_type=MESH,
        )

    def each(function):
        def step_body(step, carry):
            function(step)
            return carry

        lax.fori_loop(1, devices, step_body, 0)

    pl.semaphore_wait(barrier, devices - 1)
    for side in range(4):
        pl.when(ends[side])(lambda side=side: halo_copy(side).start())

    caps = fsend_ref.shape[0]
    slab = fault_out.shape[1]
    lines = devices * slab
    slab_shift = slab.bit_length() - 1
    widen = ((iota((devices, lines), 1) >> slab_shift) == iota((devices, lines), 0)).astype(F32)
    picks = jnp.dot(fsend_ref[...].astype(F32), widen, precision=EXACT, preferred_element_type=F32)
    part = iota((1, lines), 1) & (slab - 1)
    index = jnp.where((part & 1) == 0, picks[0:1], picks[1:2])
    hit = iota((cells, lines), 0).astype(F32) == index
    take_l = jnp.where(hit & (part < caps), 1.0, 0.0)
    take_m = jnp.where(hit & (part >= caps) & (part < 2 * caps), 1.0, 0.0)
    gathered = lax.dot_general(
        take_l, deriv, TN, precision=EXACT, preferred_element_type=F32
    ) + lax.dot_general(take_m, misc, TN, precision=EXACT, preferred_element_type=F32)
    fault_out[...] = gathered.reshape(devices, slab, LANES)
    each(lambda step: block_copy(fault_out, fault_in, fault_ssem, fault_rsem, step).start())
    fault_in[pl.ds(me, 1)] = fault_out[pl.ds(me, 1)]

    owner = owner_ref[...]
    named = (iota((devices, cells), 0) == owner).astype(F32)
    before = (iota((cells, cells), 0) < iota((cells, cells), 1)).astype(BF16)
    earlier = jnp.dot(named.astype(BF16), before, preferred_element_type=F32)
    rank = jnp.sum(earlier * named, 0, keepdims=True)
    slot = owner.astype(F32) * ROWS + rank
    slots = devices * ROWS
    mover = jnp.where(iota((slots, cells), 0).astype(F32) == slot, 1.0, 0.0).astype(BF16)

    pressure = misc[:, lane_p : lane_p + 1]
    row = iota((cells, 1), 0)
    at_x = row >> shift
    at_y = row & (width - 1)

    def terms(other_l, other_m, conduct, flag):
        lower = 1.0 - flag
        diff = pressure - other_m[:, lane_p : lane_p + 1]
        mu = conduct * (flag * misc + lower * other_m)
        off = (conduct * lower * diff) * other_l - mu
        return conduct * flag * diff, mu, off

    for side in range(4):
        @pl.when(ends[side])
        def _(side=side):
            halo_copy(side ^ 1).wait_recv()

        @pl.when(jnp.logical_not(ends[side]))
        def _(side=side):
            halo_in[side] = jnp.zeros_like(halo_in[side])

    def column(array, lane):
        return array[:, lane : lane + 1]

    near_l = jnp.concatenate([halo_in[0, 0:width], deriv[:last]], 0)
    near_m = jnp.concatenate([halo_in[0, width : 2 * width], misc[:last]], 0)
    far_l = jnp.concatenate([deriv[width:], halo_in[1, 0:width]], 0)
    far_m = jnp.concatenate([misc[width:], halo_in[1, width : 2 * width]], 0)
    for kept, field, rows, amount, start, side in (
        (lower_y_l, deriv, slice(0, width), 1, 0, 2),
        (lower_y_m, misc, slice(width, 2 * width), 1, 0, 2),
        (upper_y_l, deriv, slice(0, width), cells - 1, width - 1, 3),
        (upper_y_m, misc, slice(width, 2 * width), cells - 1, width - 1, 3),
    ):
        kept[...] = pltpu.roll(field, amount, 0)
        kept[pl.ds(start, width, stride=width), :] = halo_in[side, rows, :]

    keep_x = jnp.where((at_x < width - 1) | (tx < span_x - 1), 1.0, 0.0)
    keep_y = jnp.where((at_y < width - 1) | (ty < span_y - 1), 1.0, 0.0)
    low_y_m = lower_y_m[...]
    sides = (
        (near_l, near_m, column(near_m, lane_t), 1.0 - column(near_m, lane_w)),
        (far_l, far_m, column(misc, lane_t) * keep_x, column(misc, lane_w)),
        (
            lower_y_l[...],
            low_y_m,
            column(low_y_m, lane_t + 1),
            1.0 - column(low_y_m, lane_w + 1),
        ),
        (
            upper_y_l[...],
            upper_y_m[...],
            column(misc, lane_t + 1) * keep_y,
            column(misc, lane_w + 1),
        ),
    )
    scale = jnp.zeros((cells, 1), F32)
    mobile = jnp.zeros((cells, LANES), F32)
    offs = []
    for other_l, other_m, conduct, flag in sides:
        part_scale, mu, off = terms(other_l, other_m, conduct, flag)
        scale = scale + part_scale
        mobile = mobile + mu
        offs.append(off.astype(BF16))

    def send_rows(parts, buffer):
        moved = jnp.dot(
            mover, jnp.concatenate(parts, 1), preferred_element_type=F32
        ).astype(BF16)
        for i in range(len(parts)):
            buffer[:, i * ROWS : (i + 1) * ROWS, :] = moved[
                :, i * LANES : (i + 1) * LANES
            ].reshape(devices, ROWS, LANES)

    send_rows(offs, send_off)
    each(lambda step: block_copy(send_off, land_off, off_ssem, off_rsem, step).start())
    own_off = pltpu.make_async_copy(send_off.at[me], land_off.at[me], own_sem.at[0])
    own_off.start()

    faults = fcell_ref.shape[1]
    chosen = (iota((cells, faults), 0) == fcell_ref[...]).astype(F32)
    fslot = fslot_ref[...]
    line = lax.div(fslot, caps) * slab + lax.rem(fslot, caps)

    def of_cell(values):
        return jnp.sum(chosen * values, 1, keepdims=True)

    base = of_cell(line.astype(F32))
    conduct = of_cell(ftrans_ref[...])
    flag = of_cell(fup_ref[...].astype(F32))
    where = iota((cells, lines), 1).astype(F32)
    pull_l = jnp.where(where == base, 1.0, 0.0)
    pull_m = jnp.where(where == base + caps, 1.0, 0.0)
    each(lambda step: block_arrival(fault_out, fault_in, fault_ssem, fault_rsem, step).wait_recv())
    arrived = fault_in[...].reshape(lines, LANES)
    other_l = jnp.dot(pull_l, arrived, precision=EXACT, preferred_element_type=F32)
    other_m = jnp.dot(pull_m, arrived, precision=EXACT, preferred_element_type=F32)
    part_scale, mu, off = terms(other_l, other_m, conduct, flag)
    diag = (scale + part_scale) * deriv + (mobile + mu)
    state_m[...] = diag
    state_m[:, 0:entries] = state_m[:, 0:entries] + acc_ref[...]
    send_rows([state_m[...].astype(BF16), off.astype(BF16)], send_diag)
    each(lambda step: block_copy(send_diag, land_diag, diag_ssem, diag_rsem, step).start())
    own_diag = pltpu.make_async_copy(send_diag.at[me], land_diag.at[me], own_sem.at[1])
    own_diag.start()

    for side in range(4):
        pl.when(ends[side])(lambda side=side: halo_copy(side).wait_send())
    each(lambda step: block_copy(fault_out, fault_in, fault_ssem, fault_rsem, step).wait_send())
    each(lambda step: block_copy(send_off, land_off, off_ssem, off_rsem, step).wait_send())
    each(lambda step: block_copy(send_diag, land_diag, diag_ssem, diag_rsem, step).wait_send())
    own_off.wait()
    own_diag.wait()
    each(lambda step: block_arrival(send_off, land_off, off_ssem, off_rsem, step).wait_recv())
    each(lambda step: block_arrival(send_diag, land_diag, diag_ssem, diag_rsem, step).wait_recv())


def expand_kernel(capacity, count, off_ref, diag_ref, out_ref):
    group = off_ref.shape[0]
    parts = (off_ref.shape[1] + diag_ref.shape[1]) // ROWS
    tall = capacity * BLOCKS
    part = iota((tall, parts * ROWS), 1) // ROWS
    block = jnp.where(part < 4, part + 1, jnp.where(part == 4, 0, BLOCKS - 1))
    rank = iota((tall, parts * ROWS), 1) % ROWS
    line = iota((tall, parts * ROWS), 0)
    order = ((line // BLOCKS == rank) & (line % BLOCKS == block)).astype(BF16)
    entry = iota((LANES, PAD * PAD), 0)
    target = entry // count * PAD + entry % count
    widen = ((iota((LANES, PAD * PAD), 1) == target) & (entry < count * count)).astype(BF16)
    pieces = []
    for i in range(group):
        lines = jnp.concatenate([off_ref[i], diag_ref[i]], 0)
        pieces.append(jnp.dot(order, lines, preferred_element_type=F32).astype(BF16))
    full = jnp.dot(jnp.concatenate(pieces, 0), widen, preferred_element_type=F32)
    out_ref[...] = full.astype(BF16).reshape(group * capacity, BLOCKS, PAD * PAD)


def body(
    span_x,
    span_y,
    pressure,
    mobility,
    mob_deriv,
    accum,
    trans,
    upwind,
    fault_send,
    fault_cell,
    fault_slot,
    fault_trans,
    fault_up,
    cell_owner,
):
    width = pressure.shape[0]
    count = mobility.shape[0]
    cells = width * width
    devices = span_x * span_y
    capacity = max(2, 2 * cells // devices)
    caps = fault_send.shape[2]
    assert pressure.shape == (width, width, 1) and caps == 2
    entries = count * count
    vmem = pl.BlockSpec(memory_space=pltpu.VMEM)
    anywhere = pl.BlockSpec(memory_space=pl.ANY)
    wide = pltpu.VMEM((cells, LANES), F32)
    sems = pltpu.SemaphoreType.DMA
    land_off, land_diag = pl.pallas_call(
        functools.partial(build_kernel, span_x, span_y, width, count),
        out_shape=(
            jax.ShapeDtypeStruct((devices, 4 * ROWS, LANES), BF16),
            jax.ShapeDtypeStruct((devices, 2 * ROWS, LANES), BF16),
        ),
        in_specs=[vmem] * 12,
        out_specs=(anywhere, anywhere),
        scratch_shapes=[wide] * 6
        + [
            pltpu.VMEM((4, 2 * width, LANES), F32),
            pltpu.VMEM((4, 2 * width, LANES), F32),
            pltpu.VMEM((devices, 8, LANES), F32),
            pltpu.VMEM((devices, 8, LANES), F32),
            pltpu.VMEM((devices, 4 * ROWS, LANES), BF16),
            pltpu.VMEM((devices, 2 * ROWS, LANES), BF16),
            sems((4,)),
            sems((4,)),
            sems((devices,)),
            sems((devices,)),
            sems((devices,)),
            sems((devices,)),
            sems((devices,)),
            sems((devices,)),
            sems((2,)),
        ],
        compiler_params=pltpu.CompilerParams(
            collective_id=0, has_side_effects=True, vmem_limit_bytes=VMEM_LIMIT
        ),
        name="build_rows",
    )(
        pressure.reshape(width, width),
        mobility.reshape(count * width, width),
        jnp.transpose(mob_deriv, (1, 2, 3, 0)).reshape(cells, entries),
        jnp.transpose(accum, (1, 2, 3, 0)).reshape(cells, entries),
        trans.reshape(3 * width, width),
        upwind.reshape(3 * width, width),
        jnp.transpose(fault_send, (0, 2, 1)).reshape(caps, devices),
        fault_cell,
        fault_slot,
        fault_trans,
        fault_up,
        cell_owner.reshape(1, cells),
    )
    group = 8
    return pl.pallas_call(
        functools.partial(expand_kernel, capacity, count),
        grid=(devices // group,),
        out_shape=jax.ShapeDtypeStruct((devices * capacity, BLOCKS, PAD * PAD), BF16),
        in_specs=[
            pl.BlockSpec((group, 4 * ROWS, LANES), lambda i: (i, 0, 0)),
            pl.BlockSpec((group, 2 * ROWS, LANES), lambda i: (i, 0, 0)),
        ],
        out_specs=pl.BlockSpec((group * capacity, BLOCKS, PAD * PAD), lambda i: (i, 0, 0)),
        compiler_params=pltpu.CompilerParams(vmem_limit_bytes=VMEM_LIMIT),
        name="expand_rows",
    )(land_off, land_diag)


def solution(mesh):
    in_specs = (
        P("tx", "ty", None),
        P(None, "tx", "ty", None),
        P(None, "tx", "ty", None),
        P(None, "tx", "ty", None),
        P(None, "tx", "ty", None),
        P(None, "tx", "ty", None),
        P(("tx", "ty"), None, None),
        P(("tx", "ty"), None),
        P(("tx", "ty"), None),
        P(("tx", "ty"), None),
        P(("tx", "ty"), None),
        P(("tx", "ty"), None),
    )
    out_specs = P(("tx", "ty"), None, None)
    local = functools.partial(body, mesh.shape["tx"], mesh.shape["ty"])
    return jax.shard_map(local, mesh=mesh, in_specs=in_specs, out_specs=out_specs, check_vma=False)
```

time: 138 us -> 43.4 us (0.31); the launches traced: 136 us -> 43 us
  blocking collectives: 53.9 us -> 0 us
  local copies, waits for them, and re-layouts: 45 us -> 8.84 us
  Pallas kernels: 0 us -> 34.2 us
  starting transfers between devices: 18.6 us -> 0 us
  other arithmetic: 16 us -> 0 us
    all_to_all x1 -> x0, blocking collectives: 53.9 us -> none  [body(): lax.all_to_all(buffer.reshape(devices, capacity, -1), ('tx', 'ty'), split...]
    pallas_call x0 -> x2, Pallas kernels: none -> 34.2 us  [the longest x1 31.2 us: body(): pl.pallas_call(functools.partial(build_kernel, span_x, span_y, width, cou...]
    mul x29 -> x0, local copies, waits for them, and re-layouts: 12.9 us -> none  [the longest x10 5.46 us: direction_terms(): pressure_part = mob_up[:, None] * column]
    all_to_all x1 -> x0, starting transfers between devices: 9.34 us -> none  [body(): lax.all_to_all(outgoing.astype(jnp.bfloat16), ('tx', 'ty'), split_axis=1,...]
    ppermute x4 -> x0, starting transfers between devices: 9.31 us -> none  [the longest x2 6.56 us: with_halo(): lax.ppermute(tail, axis, [(i, (i + 1) % count) for i in range(ends)])]
    reshape x8 -> x0, local copies, waits for them, and re-layouts: 7.04 us -> none  [the longest x4 4.07 us: direction_terms(): deriv_other = state_other[count + 1:].reshape((count, count) + rest)]
    ppermute x2 -> x0, local copies, waits for them, and re-layouts: 4.56 us -> none  [the longest x1 2.83 us: with_halo(): lax.ppermute(head, axis, [((i + 1) % count, i) for i in range(ends)])]
    concatenate x4 -> x0, other arithmetic: 4.02 us -> none  [the longest x3 3.82 us: with_halo(): jnp.concatenate([lax.ppermute(tail, axis, [(i, (i + 1) % count) for i in...]
  transfers between devices with their start and end apart: 5 -> 0, of which waited for: 0 -> 0; matrix products, arithmetic and copies ran while one was open for 34% -> 0% of each run, Pallas kernels for 0% -> 0%
where the time goes in v1:
time: 43.4 us; the launch traced here: 43 us
  Pallas kernels  34.2 us (79%)
  local copies, waits for them, and re-layouts  8.84 us (20%)
    pallas_call x1, Pallas kernels, body(): pl.pallas_call(functools.partial(build_kernel, span_x, span_y, width, cou...  31.2 us
    unnamed x24, local copies, waits for them, and re-layouts  8.84 us
    pallas_call x1, Pallas kernels, body(): pl.pallas_call(functools.partial(expand_kernel, capacity, count), grid=(d...  2.91 us

profile of v1, /device:TPU:0, one launch (start us, length us, event | category | flops | bytes accessed | tf_op | source)
XLA Modules:
  0.0 43.0 jit_solution(12813056391172538695)
XLA Ops:
  0.0 0.0 copy-start
  0.0 0.9 %copy-done = f32[121,16,16,1]{0,3,2,1:T(1,128)S(1)} copy-done((f32[121,16,16,1]{0,3,2,1:T(1,128)S(1)}, f32[121,16,16,1]{0,3,2,1:T(1,128)}, u32[]{:S(2)}) %copy-start) | copy-done | bytes 123928
  0.9 0.0 copy-start.1
  0.9 0.9 %copy-done.1 = f32[121,16,16,1]{0,3,2,1:T(1,128)S(1)} copy-done((f32[121,16,16,1]{0,3,2,1:T(1,128)S(1)}, f32[121,16,16,1]{0,3,2,1:T(1,128)}, u32[]{:S(2)}) %copy-start.1) | copy-done | bytes 123928
  1.8 0.0 copy-start.2
  1.8 0.9 %copy-done.2 = f32[11,16,16,1]{2,3,1,0:T(1,128)S(1)} copy-done((f32[11,16,16,1]{2,3,1,0:T(1,128)S(1)}, f32[11,16,16,1]{2,3,1,0:T(1,128)}, u32[]{:S(2)}) %copy-start.2) | copy-done | bytes 11288
  2.7 0.0 copy-start.3
  2.7 0.7 %copy-done.3 = f32[3,16,16,1]{2,3,1,0:T(1,128)S(1)} copy-done((f32[3,16,16,1]{2,3,1,0:T(1,128)S(1)}, f32[3,16,16,1]{2,3,1,0:T(1,128)}, u32[]{:S(2)}) %copy-start.3) | copy-done | bytes 3096
  3.4 0.0 copy-start.4
  3.4 0.7 %copy-done.4 = s32[3,16,16,1]{2,3,1,0:T(1,128)S(1)} copy-done((s32[3,16,16,1]{2,3,1,0:T(1,128)S(1)}, s32[3,16,16,1]{2,3,1,0:T(1,128)}, u32[]{:S(2)}) %copy-start.4) | copy-done | bytes 3096
  4.2 0.0 copy-start.5
  4.2 0.7 %copy-done.5 = f32[16,16,1]{1,2,0:T(1,128)S(1)} copy-done((f32[16,16,1]{1,2,0:T(1,128)S(1)}, f32[16,16,1]{1,2,0:T(1,128)}, u32[]{:S(2)}) %copy-start.5) | copy-done | bytes 1048
  4.9 0.0 copy-start.6
  4.9 0.7 %copy-done.6 = s32[1,32,2]{1,2,0:T(2,128)S(1)} copy-done((s32[1,32,2]{1,2,0:T(2,128)S(1)}, s32[1,32,2]{1,2,0:T(2,128)}, u32[]{:S(2)}) %copy-start.6) | copy-done | bytes 280
  5.6 0.0 copy-start.7
  5.6 0.7 %copy-done.7 = s32[256,1]{0,1:T(1,128)S(1)} copy-done((s32[256,1]{0,1:T(1,128)S(1)}, s32[256,1]{0,1:T(1,128)}, u32[]{:S(2)}) %copy-start.7) | copy-done | bytes 1048
  6.2 0.0 copy-start.8
  6.2 0.7 %copy-done.8 = s32[1,64]{1,0:T(1,128)S(1)} copy-done((s32[1,64]{1,0:T(1,128)S(1)}, s32[1,64]{1,0:T(1,128)}, u32[]{:S(2)}) %copy-start.8) | copy-done | bytes 280
  6.9 0.0 copy-start.9
  6.9 0.7 %copy-done.9 = s32[1,64]{1,0:T(1,128)S(1)} copy-done((s32[1,64]{1,0:T(1,128)S(1)}, s32[1,64]{1,0:T(1,128)}, u32[]{:S(2)}) %copy-start.9) | copy-done | bytes 280
  7.5 0.0 copy-start.10
  7.5 0.7 %copy-done.10 = f32[1,64]{1,0:T(1,128)S(1)} copy-done((f32[1,64]{1,0:T(1,128)S(1)}, f32[1,64]{1,0:T(1,128)}, u32[]{:S(2)}) %copy-start.10) | copy-done | bytes 280
  8.2 0.0 copy-start.11
  8.2 0.7 %copy-done.11 = s32[1,64]{1,0:T(1,128)S(1)} copy-done((s32[1,64]{1,0:T(1,128)S(1)}, s32[1,64]{1,0:T(1,128)}, u32[]{:S(2)}) %copy-start.11) | copy-done | bytes 280
  8.9 31.2 %build_rows.1 = (bf16[32,64,128]{2,1,0:T(8,128)(2,1)S(1)}, bf16[32,32,128]{2,1,0:T(8,128)(2,1)S(1)}) custom-call(f32[16,16]{1,0:T(8,128)S(1)} %bitcast.19, f32[176,16]{1,0:T(8,128)S(1)} %bitcast.16, f32[256,121]{1,0:T(8,128)S(1)} %bitcast.14, f32[256,121]{1,0:T(8,128)S(1)} %bitcast.15, f32[48,16]{1,0:T(8,128)S(1)} %bitcast.17, s32[48,16]{1,0:T(8,128)S(1)} %bitcast.18, ...), custom_call_target="tpu_custom_call" | custom-call | tf_op jit(solution)/shard_map/build_rows/pallas_call | solution.py:368
  40.1 2.9 %expand_rows.1 = bf16[512,8,256]{2,1,0:T(8,128)(2,1)} custom-call(bf16[32,64,128]{2,1,0:T(8,128)(2,1)S(1)} %get-tuple-element.7.off_ref, bf16[32,32,128]{2,1,0:T(8,128)(2,1)S(1)} %get-tuple-element.8.diag_ref), custom_call_target="tpu_custom_call" | custom-call | tf_op jit(solution)/shard_map/expand_rows/pallas_call | solution.py:413
Async XLA Ops:
  0.0 0.9 %copy-start = (f32[121,16,16,1]{0,3,2,1:T(1,128)S(1)}, f32[121,16,16,1]{0,3,2,1:T(1,128)}, u32[]{:S(2)}) copy-start(f32[121,16,16,1]{0,3,2,1:T(1,128)} %param.14) | copy-start | bytes 371716
  0.9 0.9 %copy-start.1 = (f32[121,16,16,1]{0,3,2,1:T(1,128)S(1)}, f32[121,16,16,1]{0,3,2,1:T(1,128)}, u32[]{:S(2)}) copy-start(f32[121,16,16,1]{0,3,2,1:T(1,128)} %param.15) | copy-start | bytes 371716
  1.8 0.9 %copy-start.2 = (f32[11,16,16,1]{2,3,1,0:T(1,128)S(1)}, f32[11,16,16,1]{2,3,1,0:T(1,128)}, u32[]{:S(2)}) copy-start(f32[11,16,16,1]{2,3,1,0:T(1,128)} %param.13) | copy-start | bytes 33796
  2.7 0.7 %copy-start.3 = (f32[3,16,16,1]{2,3,1,0:T(1,128)S(1)}, f32[3,16,16,1]{2,3,1,0:T(1,128)}, u32[]{:S(2)}) copy-start(f32[3,16,16,1]{2,3,1,0:T(1,128)} %param.16) | copy-start | bytes 9220
  3.4 0.7 %copy-start.4 = (s32[3,16,16,1]{2,3,1,0:T(1,128)S(1)}, s32[3,16,16,1]{2,3,1,0:T(1,128)}, u32[]{:S(2)}) copy-start(s32[3,16,16,1]{2,3,1,0:T(1,128)} %param.17) | copy-start | bytes 9220
  4.2 0.7 %copy-start.5 = (f32[16,16,1]{1,2,0:T(1,128)S(1)}, f32[16,16,1]{1,2,0:T(1,128)}, u32[]{:S(2)}) copy-start(f32[16,16,1]{1,2,0:T(1,128)} %param.12) | copy-start | bytes 3076
  4.9 0.7 %copy-start.6 = (s32[1,32,2]{1,2,0:T(2,128)S(1)}, s32[1,32,2]{1,2,0:T(2,128)}, u32[]{:S(2)}) copy-start(s32[1,32,2]{1,2,0:T(2,128)} %param.18) | copy-start | bytes 772
  5.6 0.7 %copy-start.7 = (s32[256,1]{0,1:T(1,128)S(1)}, s32[256,1]{0,1:T(1,128)}, u32[]{:S(2)}) copy-start(s32[256,1]{0,1:T(1,128)} %param.23) | copy-start | bytes 3076
  6.2 0.7 %copy-start.8 = (s32[1,64]{1,0:T(1,128)S(1)}, s32[1,64]{1,0:T(1,128)}, u32[]{:S(2)}) copy-start(s32[1,64]{1,0:T(1,128)} %fcell_ref.1) | copy-start | bytes 772
  6.9 0.7 %copy-start.9 = (s32[1,64]{1,0:T(1,128)S(1)}, s32[1,64]{1,0:T(1,128)}, u32[]{:S(2)}) copy-start(s32[1,64]{1,0:T(1,128)} %fslot_ref.1) | copy-start | bytes 772
  7.5 0.7 %copy-start.10 = (f32[1,64]{1,0:T(1,128)S(1)}, f32[1,64]{1,0:T(1,128)}, u32[]{:S(2)}) copy-start(f32[1,64]{1,0:T(1,128)} %ftrans_ref.1) | copy-start | bytes 772
  8.2 0.7 %copy-start.11 = (s32[1,64]{1,0:T(1,128)S(1)}, s32[1,64]{1,0:T(1,128)}, u32[]{:S(2)}) copy-start(s32[1,64]{1,0:T(1,128)} %fup_ref.1) | copy-start | bytes 772

commit v2 on v1

v2 whole, which is shorter than its diff:
```python
import functools

import jax
import jax.numpy as jnp
from jax import lax
from jax.experimental import pallas as pl
from jax.experimental.pallas import tpu as pltpu
from jax.sharding import PartitionSpec as P

PAD = 16
BLOCKS = 8
LANES = 128
ROWS = 16
MESH = pl.DeviceIdType.MESH
F32 = jnp.float32
BF16 = jnp.bfloat16
NT = (((1,), (1,)), ((), ()))
VMEM_LIMIT = 60 * 1024 * 1024


def iota(shape, dim):
    return lax.broadcasted_iota(jnp.int32, shape, dim)


def split(values, terms):
    pieces = []
    for _ in range(terms - 1):
        pieces.append(values.astype(BF16))
        values = values - pieces[-1].astype(F32)
    return pieces + [values.astype(BF16)]


def joined(values, terms):
    total = values[:, 0:LANES]
    for i in range(1, terms):
        total = total + values[:, i * LANES : (i + 1) * LANES]
    return total


def one_hot(mask):
    return jnp.where(mask, 1.0, 0.0).astype(BF16)


def build_kernel(
    span_x,
    span_y,
    width,
    count,
    *refs,
):
    sources, refs = refs[:12], refs[12:]
    land_off, land_diag = refs[:2]
    inputs, refs = refs[2:14], refs[14:]
    (
        p_ref,
        m_ref,
        deriv_ref,
        acc_ref,
        trans_ref,
        up_ref,
        fsend_ref,
        fcell_ref,
        fslot_ref,
        ftrans_ref,
        fup_ref,
        owner_ref,
    ) = inputs
    (
        state_l,
        state_m,
        lower_y_l,
        lower_y_m,
        upper_y_l,
        upper_y_m,
        halo_out,
        halo_in,
        fault_out,
        fault_in,
        send_off,
        send_diag,
        input_sem,
        halo_ssem,
        halo_rsem,
        block_ssem,
        block_rsem,
        own_sem,
    ) = refs
    devices = span_x * span_y
    cells = width * width
    entries = count * count
    shift = width.bit_length() - 1
    lane_p, lane_t, lane_w = entries, entries + 1, entries + 3
    tx = lax.axis_index("tx")
    ty = lax.axis_index("ty")
    me = tx * span_y + ty

    loads = [
        pltpu.make_async_copy(source, target, input_sem.at[i])
        for i, (source, target) in enumerate(zip(sources, inputs))
    ]
    for load in loads:
        load.start()

    flips = []
    for code in range(span_y - 1, -1, -1):
        flipped = ty
        for bit in range(span_y.bit_length() - 1):
            if code >> bit & 1:
                flipped = flipped + (1 - 2 * (ty // (1 << bit) % 2)) * (1 << bit)
        flips.append(flipped)

    def each(function):
        def column_of(codes, step):
            x = tx + step
            x = x - jnp.where(x >= span_x, span_x, 0)
            for y in codes:
                function(x, y)

        def run(codes):
            def step_body(step, carry):
                column_of(codes, step)
                return carry

            lax.fori_loop(1, span_x, step_body, 0)

        half = span_y // 2
        column_of(flips[:half], 0)
        run(flips[:half])
        column_of(flips[half : span_y - 1], 0)
        run(flips[half:])

    barrier = pltpu.get_barrier_semaphore()
    each(
        lambda x, y: pl.semaphore_signal(
            barrier, inc=1, device_id=(x, y), device_id_type=MESH
        )
    )

    def send_all(src, dst, kind):
        each(
            lambda x, y: pltpu.make_async_remote_copy(
                src_ref=src.at[x * span_y + y],
                dst_ref=dst.at[me],
                send_sem=block_ssem.at[kind],
                recv_sem=block_rsem.at[kind],
                device_id=(x, y),
                device_id_type=MESH,
            ).start()
        )

    def await_all(buffer, sem):
        span = buffer.at[pl.ds(0, devices - 1)]
        pltpu.make_async_copy(span, span, sem).wait()

    for load in loads:
        load.wait()

    fields = jnp.concatenate(
        [
            p_ref[...],
            m_ref[...],
            trans_ref[0 : 2 * width, :],
            up_ref[0 : 2 * width, :].astype(F32),
        ],
        0,
    )
    nfield = fields.shape[0]
    spread = one_hot((iota((cells, width), 0) & (width - 1)) == iota((cells, width), 1))
    crossed = lax.dot_general(
        jnp.concatenate([spread] * 3, 1),
        jnp.concatenate(split(fields, 3), 1),
        NT,
        preferred_element_type=F32,
    )
    same = (iota((cells, nfield), 1) & (width - 1)) == (iota((cells, nfield), 0) >> shift)
    kind = iota((nfield, LANES), 0) >> shift
    lane_of = jnp.where(
        kind == 0,
        lane_p,
        jnp.where(kind <= count, (kind - 1) * count, kind - (count + 1) + lane_t),
    )
    sorter = one_hot(iota((nfield, LANES), 1) == lane_of)
    misc = jnp.dot(
        jnp.concatenate(split(jnp.where(same, crossed, 0.0), 3), 1),
        jnp.concatenate([sorter] * 3, 0),
        preferred_element_type=F32,
    )
    state_m[...] = misc
    state_l[...] = jnp.zeros_like(state_l)
    state_l[:, 0:entries] = deriv_ref[...]
    deriv = state_l[...]

    last = cells - width
    halo_out[0, 0:width] = deriv[0:width]
    halo_out[0, width : 2 * width] = misc[0:width]
    halo_out[1, 0:width] = deriv[last:]
    halo_out[1, width : 2 * width] = misc[last:]
    for side, start in ((2, 0), (3, width - 1)):
        halo_out[side, 0:width] = state_l[pl.ds(start, width, stride=width), :]
        halo_out[side, width : 2 * width] = state_m[pl.ds(start, width, stride=width), :]

    ends = (tx > 0, tx < span_x - 1, ty > 0, ty < span_y - 1)
    targets = ((tx - 1, ty), (tx + 1, ty), (tx, ty - 1), (tx, ty + 1))

    def halo_copy(side):
        return pltpu.make_async_remote_copy(
            src_ref=halo_out.at[side],
            dst_ref=halo_in.at[side ^ 1],
            send_sem=halo_ssem.at[side],
            recv_sem=halo_rsem.at[side ^ 1],
            device_id=targets[side],
            device_id_type=MESH,
        )

    caps = fsend_ref.shape[0]
    slab = fault_out.shape[1]
    lines = devices * slab
    slab_shift = slab.bit_length() - 1
    widen = one_hot((iota((lines, devices), 0) >> slab_shift) == iota((lines, devices), 1))
    picks = lax.dot_general(
        widen, fsend_ref[...].astype(F32).astype(BF16), NT, preferred_element_type=F32
    )
    part = iota((lines, 1), 0) & (slab - 1)
    index = jnp.where((part & 1) == 0, picks[:, 0:1], picks[:, 1:2])
    hit = iota((lines, cells), 1).astype(F32) == index
    take_l = one_hot(hit & (part < caps))
    take_m = one_hot(hit & (part >= caps) & (part < 2 * caps))
    gathered = joined(
        jnp.dot(take_l, jnp.concatenate(split(deriv, 2), 1), preferred_element_type=F32), 2
    ) + joined(
        jnp.dot(take_m, jnp.concatenate(split(misc, 3), 1), preferred_element_type=F32), 3
    )
    fault_out[...] = gathered.reshape(devices, slab, LANES)
    fault_in[pl.ds(me, 1)] = fault_out[pl.ds(me, 1)]

    pl.semaphore_wait(barrier, devices - 1)
    for side in range(4):
        pl.when(ends[side])(lambda side=side: halo_copy(side).start())
    send_all(fault_out, fault_in, 0)

    owner = owner_ref[...]
    named = (iota((devices, cells), 0) == owner).astype(F32)
    before = one_hot(iota((cells, cells), 0) < iota((cells, cells), 1))
    earlier = jnp.dot(named.astype(BF16), before, preferred_element_type=F32)
    rank = jnp.sum(earlier * named, 0, keepdims=True)
    slot = owner.astype(F32) * ROWS + rank
    slots = devices * ROWS
    mover = one_hot(iota((slots, cells), 0).astype(F32) == slot)

    faults = fcell_ref.shape[1]
    chosen = (iota((cells, faults), 0) == fcell_ref[...]).astype(F32)
    fslot = fslot_ref[...]
    line = lax.div(fslot, caps) * slab + lax.rem(fslot, caps)

    def of_cell(values):
        return jnp.sum(chosen * values, 1, keepdims=True)

    base = of_cell(line.astype(F32))
    fault_conduct = of_cell(ftrans_ref[...])
    fault_flag = of_cell(fup_ref[...].astype(F32))
    where = iota((cells, lines), 1).astype(F32)
    pull_l = one_hot(where == base)
    pull_m = one_hot(where == base + caps)

    pressure = misc[:, lane_p : lane_p + 1]
    row = iota((cells, 1), 0)
    at_x = row >> shift
    at_y = row & (width - 1)

    def terms(other_l, other_m, conduct, flag):
        lower = 1.0 - flag
        diff = pressure - other_m[:, lane_p : lane_p + 1]
        mu = (conduct * flag) * misc + (conduct * lower) * other_m
        off = (conduct * lower * diff) * other_l - mu
        return conduct * flag * diff, mu, off

    for side in range(4):
        @pl.when(ends[side])
        def _(side=side):
            halo_copy(side ^ 1).wait_recv()

        @pl.when(jnp.logical_not(ends[side]))
        def _(side=side):
            halo_in[side] = jnp.zeros_like(halo_in[side])

    def column(array, lane):
        return array[:, lane : lane + 1]

    near_l = jnp.concatenate([halo_in[0, 0:width], deriv[:last]], 0)
    near_m = jnp.concatenate([halo_in[0, width : 2 * width], misc[:last]], 0)
    far_l = jnp.concatenate([deriv[width:], halo_in[1, 0:width]], 0)
    far_m = jnp.concatenate([misc[width:], halo_in[1, width : 2 * width]], 0)
    for kept, field, rows, amount, start, side in (
        (lower_y_l, deriv, slice(0, width), 1, 0, 2),
        (lower_y_m, misc, slice(width, 2 * width), 1, 0, 2),
        (upper_y_l, deriv, slice(0, width), cells - 1, width - 1, 3),
        (upper_y_m, misc, slice(width, 2 * width), cells - 1, width - 1, 3),
    ):
        kept[...] = pltpu.roll(field, amount, 0)
        kept[pl.ds(start, width, stride=width), :] = halo_in[side, rows, :]

    keep_x = jnp.where((at_x < width - 1) | (tx < span_x - 1), 1.0, 0.0)
    keep_y = jnp.where((at_y < width - 1) | (ty < span_y - 1), 1.0, 0.0)
    low_y_m = lower_y_m[...]
    sides = (
        (near_l, near_m, column(near_m, lane_t), 1.0 - column(near_m, lane_w)),
        (far_l, far_m, column(misc, lane_t) * keep_x, column(misc, lane_w)),
        (
            lower_y_l[...],
            low_y_m,
            column(low_y_m, lane_t + 1),
            1.0 - column(low_y_m, lane_w + 1),
        ),
        (
            upper_y_l[...],
            upper_y_m[...],
            column(misc, lane_t + 1) * keep_y,
            column(misc, lane_w + 1),
        ),
    )
    scale = jnp.zeros((cells, 1), F32)
    mobile = jnp.zeros((cells, LANES), F32)
    offs = []
    for other_l, other_m, conduct, flag in sides:
        part_scale, mu, off = terms(other_l, other_m, conduct, flag)
        scale = scale + part_scale
        mobile = mobile + mu
        offs.append(off.astype(BF16))

    def place_rows(parts, buffer):
        moved = jnp.dot(
            mover, jnp.concatenate(parts, 1), preferred_element_type=F32
        ).astype(BF16)
        for i in range(len(parts)):
            buffer[:, i * ROWS : (i + 1) * ROWS, :] = moved[
                :, i * LANES : (i + 1) * LANES
            ].reshape(devices, ROWS, LANES)

    place_rows(offs, send_off)
    send_all(send_off, land_off, 1)
    own_off = pltpu.make_async_copy(send_off.at[me], land_off.at[me], own_sem.at[0])
    own_off.start()

    await_all(fault_in, block_rsem.at[0])
    arrived = fault_in[...].reshape(lines, LANES)
    pieces = split(arrived, 3)
    other_l = joined(
        jnp.dot(pull_l, jnp.concatenate(pieces[:2], 1), preferred_element_type=F32), 2
    )
    other_m = joined(
        jnp.dot(pull_m, jnp.concatenate(pieces, 1), preferred_element_type=F32), 3
    )
    part_scale, mu, off = terms(other_l, other_m, fault_conduct, fault_flag)
    diag = (scale + part_scale) * deriv + (mobile + mu)
    state_m[...] = diag
    state_m[:, 0:entries] = state_m[:, 0:entries] + acc_ref[...]
    place_rows([state_m[...].astype(BF16), off.astype(BF16)], send_diag)
    send_all(send_diag, land_diag, 2)
    own_diag = pltpu.make_async_copy(send_diag.at[me], land_diag.at[me], own_sem.at[1])
    own_diag.start()

    for side in range(4):
        pl.when(ends[side])(lambda side=side: halo_copy(side).wait_send())
    await_all(fault_out, block_ssem.at[0])
    await_all(send_off, block_ssem.at[1])
    await_all(send_diag, block_ssem.at[2])
    own_off.wait()
    own_diag.wait()
    await_all(land_off, block_rsem.at[1])
    await_all(land_diag, block_rsem.at[2])


def expand_kernel(capacity, count, off_ref, diag_ref, out_ref, wide_ref):
    group = off_ref.shape[0]
    tall = capacity * BLOCKS
    entry = iota((LANES, PAD * PAD), 0)
    target = entry // count * PAD + entry % count
    widen = one_hot((iota((LANES, PAD * PAD), 1) == target) & (entry < count * count))
    for ref, blocks in ((off_ref, (1, 2, 3, 4)), (diag_ref, (0, BLOCKS - 1))):
        lines = ref[...].reshape(group * len(blocks) * ROWS, LANES)
        full = jnp.dot(lines, widen, preferred_element_type=F32)
        for i in range(group):
            for j, block in enumerate(blocks):
                start = (i * len(blocks) + j) * ROWS
                for half in range(2):
                    wide_ref[half, pl.ds(i * tall + block, capacity, stride=BLOCKS), :] = full[
                        start : start + capacity, half * LANES : (half + 1) * LANES
                    ]
    gap = jnp.zeros((group * capacity, LANES), F32)
    for block in (5, 6):
        for half in range(2):
            wide_ref[half, pl.ds(block, group * capacity, stride=BLOCKS), :] = gap
    for half in range(2):
        out_ref[:, :, half * LANES : (half + 1) * LANES] = (
            wide_ref[half].astype(BF16).reshape(group * capacity, BLOCKS, LANES)
        )


def body(
    span_x,
    span_y,
    pressure,
    mobility,
    mob_deriv,
    accum,
    trans,
    upwind,
    fault_send,
    fault_cell,
    fault_slot,
    fault_trans,
    fault_up,
    cell_owner,
):
    width = pressure.shape[0]
    count = mobility.shape[0]
    cells = width * width
    devices = span_x * span_y
    capacity = max(2, 2 * cells // devices)
    caps = fault_send.shape[2]
    assert pressure.shape == (width, width, 1) and caps == 2
    entries = count * count
    anywhere = pl.BlockSpec(memory_space=pl.ANY)
    wide = pltpu.VMEM((cells, LANES), F32)
    sems = pltpu.SemaphoreType.DMA
    arrays = (
        pressure.reshape(width, width),
        mobility.reshape(count * width, width),
        jnp.transpose(mob_deriv, (1, 2, 3, 0)).reshape(cells, entries),
        jnp.transpose(accum, (1, 2, 3, 0)).reshape(cells, entries),
        trans.reshape(3 * width, width),
        upwind.reshape(3 * width, width),
        jnp.transpose(fault_send, (0, 2, 1)).reshape(caps, devices),
        fault_cell,
        fault_slot,
        fault_trans,
        fault_up,
        cell_owner.reshape(1, cells),
    )
    land_off, land_diag = pl.pallas_call(
        functools.partial(build_kernel, span_x, span_y, width, count),
        out_shape=(
            jax.ShapeDtypeStruct((devices, 4 * ROWS, LANES), BF16),
            jax.ShapeDtypeStruct((devices, 2 * ROWS, LANES), BF16),
        ),
        in_specs=[pl.BlockSpec(memory_space=pltpu.HBM)] * 12,
        out_specs=(anywhere, anywhere),
        scratch_shapes=[pltpu.VMEM(array.shape, array.dtype) for array in arrays]
        + [wide] * 6
        + [
            pltpu.VMEM((4, 2 * width, LANES), F32),
            pltpu.VMEM((4, 2 * width, LANES), F32),
            pltpu.VMEM((devices, 8, LANES), F32),
            pltpu.VMEM((devices, 8, LANES), F32),
            pltpu.VMEM((devices, 4 * ROWS, LANES), BF16),
            pltpu.VMEM((devices, 2 * ROWS, LANES), BF16),
            sems((len(arrays),)),
            sems((4,)),
            sems((4,)),
            sems((3,)),
            sems((3,)),
            sems((2,)),
        ],
        compiler_params=pltpu.CompilerParams(
            collective_id=0, has_side_effects=True, vmem_limit_bytes=VMEM_LIMIT
        ),
        name="build_rows",
    )(*arrays)
    group = 8
    return pl.pallas_call(
        functools.partial(expand_kernel, capacity, count),
        grid=(devices // group,),
        out_shape=jax.ShapeDtypeStruct((devices * capacity, BLOCKS, PAD * PAD), BF16),
        in_specs=[
            pl.BlockSpec((group, 4 * ROWS, LANES), lambda i: (i, 0, 0)),
            pl.BlockSpec((group, 2 * ROWS, LANES), lambda i: (i, 0, 0)),
        ],
        out_specs=pl.BlockSpec((group * capacity, BLOCKS, PAD * PAD), lambda i: (i, 0, 0)),
        scratch_shapes=[pltpu.VMEM((2, group * capacity * BLOCKS, LANES), F32)],
        compiler_params=pltpu.CompilerParams(vmem_limit_bytes=VMEM_LIMIT),
        name="expand_rows",
    )(land_off, land_diag)


def solution(mesh):
    in_specs = (
        P("tx", "ty", None),
        P(None, "tx", "ty", None),
        P(None, "tx", "ty", None),
        P(None, "tx", "ty", None),
        P(None, "tx", "ty", None),
        P(None, "tx", "ty", None),
        P(("tx", "ty"), None, None),
        P(("tx", "ty"), None),
        P(("tx", "ty"), None),
        P(("tx", "ty"), None),
        P(("tx", "ty"), None),
        P(("tx", "ty"), None),
    )
    out_specs = P(("tx", "ty"), None, None)
    local = functools.partial(body, mesh.shape["tx"], mesh.shape["ty"])
    return jax.shard_map(local, mesh=mesh, in_specs=in_specs, out_specs=out_specs, check_vma=False)
```

time: 43.4 us -> 34.6 us (0.80)
  local copies, waits for them, and re-layouts: 8.84 us -> 0 us
    unnamed x24 -> x0, local copies, waits for them, and re-layouts: 8.84 us -> none
    pallas_call x1, Pallas kernels: 2.91 us -> 4.29 us  [body(): pl.pallas_call(functools.partial(expand_kernel, capacity, count), grid=(d...]
    pallas_call x1, Pallas kernels: 31.2 us -> 30.1 us  [body(): pl.pallas_call(functools.partial(build_kernel, span_x, span_y, width, cou...]
where the time goes in v2:
time: 34.6 us; the launch traced here: 34.4 us
  Pallas kernels  34.4 us (99%)
    pallas_call x1, Pallas kernels, body(): pl.pallas_call(functools.partial(build_kernel, span_x, span_y, width, cou...  30.1 us
    pallas_call x1, Pallas kernels, body(): pl.pallas_call(functools.partial(expand_kernel, capacity, count), grid=(d...  4.29 us

profile of v2, /device:TPU:0, one launch (start us, length us, event | category | flops | bytes accessed | tf_op | source)
XLA Modules:
  0.0 34.4 jit_solution(1601203278715935866)
XLA Ops:
  0.0 30.1 %build_rows.1 = (bf16[32,64,128]{2,1,0:T(8,128)(2,1)}, bf16[32,32,128]{2,1,0:T(8,128)(2,1)}) custom-call(f32[16,16]{1,0:T(8,128)} %bitcast.19, f32[176,16]{1,0:T(8,128)} %bitcast.16, f32[256,121]{1,0:T(8,128)} %bitcast.14, f32[256,121]{1,0:T(8,128)} %bitcast.15, f32[48,16]{1,0:T(8,128)} %bitcast.17, s32[48,16]{1,0:T(8,128)} %bitcast.18, s32[2,32]{1,0:T(2,128)} %bitcast.20, ...), custom_call_target="tpu_custom_call" | custom-call | tf_op jit(solution)/shard_map/build_rows/pallas_call | solution.py:440
  30.1 4.3 %expand_rows.1 = bf16[512,8,256]{2,1,0:T(8,128)(2,1)} custom-call(bf16[32,64,128]{2,1,0:T(8,128)(2,1)} %get-tuple-element.7.off_ref, bf16[32,32,128]{2,1,0:T(8,128)(2,1)} %get-tuple-element.8.diag_ref), custom_call_target="tpu_custom_call" | custom-call | tf_op jit(solution)/shard_map/expand_rows/pallas_call | solution.py:470

commit v3 on v2

--- a/solution.py
+++ b/solution.py
@@ -212,6 +212,10 @@
             device_id_type=MESH,
         )
 
+    pl.semaphore_wait(barrier, devices - 1)
+    for side in range(4):
+        pl.when(ends[side])(lambda side=side: halo_copy(side).start())
+
     caps = fsend_ref.shape[0]
     slab = fault_out.shape[1]
     lines = devices * slab
@@ -224,7 +228,7 @@
     index = jnp.where((part & 1) == 0, picks[:, 0:1], picks[:, 1:2])
     hit = iota((lines, cells), 1).astype(F32) == index
     take_l = one_hot(hit & (part < caps))
-    take_m = one_hot(hit & (part >= caps) & (part < 2 * caps))
+    take_m = one_hot(hit & (part >= caps))
     gathered = joined(
         jnp.dot(take_l, jnp.concatenate(split(deriv, 2), 1), preferred_element_type=F32), 2
     ) + joined(
@@ -233,9 +237,6 @@
     fault_out[...] = gathered.reshape(devices, slab, LANES)
     fault_in[pl.ds(me, 1)] = fault_out[pl.ds(me, 1)]
 
-    pl.semaphore_wait(barrier, devices - 1)
-    for side in range(4):
-        pl.when(ends[side])(lambda side=side: halo_copy(side).start())
     send_all(fault_out, fault_in, 0)
 
     owner = owner_ref[...]
@@ -370,30 +371,52 @@
     await_all(land_diag, block_rsem.at[2])
 
 
-def expand_kernel(capacity, count, off_ref, diag_ref, out_ref, wide_ref):
-    group = off_ref.shape[0]
+def expand_kernel(capacity, count, group, off_hbm, diag_hbm, out_hbm, off_ref, diag_ref, out_ref, in_sem, out_sem):
+    devices = off_hbm.shape[0]
+    pieces = devices // group
+    fetches = []
+    for i in range(pieces):
+        part = pl.ds(i * group, group)
+        fetches.append(
+            (
+                pltpu.make_async_copy(off_hbm.at[part], off_ref.at[part], in_sem.at[0, i]),
+                pltpu.make_async_copy(diag_hbm.at[part], diag_ref.at[part], in_sem.at[1, i]),
+            )
+        )
+        for fetch in fetches[-1]:
+            fetch.start()
+    kinds = (off_ref.shape[1] + diag_ref.shape[1]) // ROWS
     tall = capacity * BLOCKS
+    kind = iota((tall, kinds * ROWS), 1) // ROWS
+    block = jnp.where(kind < 4, kind + 1, jnp.where(kind == 4, 0, BLOCKS - 1))
+    rank = iota((tall, kinds * ROWS), 1) % ROWS
+    line = iota((tall, kinds * ROWS), 0)
+    order = one_hot((line // BLOCKS == rank) & (line % BLOCKS == block))
     entry = iota((LANES, PAD * PAD), 0)
     target = entry // count * PAD + entry % count
     widen = one_hot((iota((LANES, PAD * PAD), 1) == target) & (entry < count * count))
-    for ref, blocks in ((off_ref, (1, 2, 3, 4)), (diag_ref, (0, BLOCKS - 1))):
-        lines = ref[...].reshape(group * len(blocks) * ROWS, LANES)
-        full = jnp.dot(lines, widen, preferred_element_type=F32)
-        for i in range(group):
-            for j, block in enumerate(blocks):
-                start = (i * len(blocks) + j) * ROWS
-                for half in range(2):
-                    wide_ref[half, pl.ds(i * tall + block, capacity, stride=BLOCKS), :] = full[
-                        start : start + capacity, half * LANES : (half + 1) * LANES
-                    ]
-    gap = jnp.zeros((group * capacity, LANES), F32)
-    for block in (5, 6):
-        for half in range(2):
-            wide_ref[half, pl.ds(block, group * capacity, stride=BLOCKS), :] = gap
-    for half in range(2):
-        out_ref[:, :, half * LANES : (half + 1) * LANES] = (
-            wide_ref[half].astype(BF16).reshape(group * capacity, BLOCKS, LANES)
-        )
+    stores = []
+    for i in range(pieces):
+        for fetch in fetches[i]:
+            fetch.wait()
+        ordered = []
+        for j in range(i * group, (i + 1) * group, 2):
+            pair = jnp.concatenate(
+                [
+                    jnp.concatenate([off_ref[j], off_ref[j + 1]], 1),
+                    jnp.concatenate([diag_ref[j], diag_ref[j + 1]], 1),
+                ],
+                0,
+            )
+            both = jnp.dot(order, pair, preferred_element_type=F32).astype(BF16)
+            ordered += [both[:, :LANES], both[:, LANES:]]
+        full = jnp.dot(jnp.concatenate(ordered, 0), widen, preferred_element_type=F32)
+        rows = pl.ds(i * group * capacity, group * capacity)
+        out_ref[rows] = full.astype(BF16).reshape(group * capacity, BLOCKS, PAD * PAD)
+        stores.append(pltpu.make_async_copy(out_ref.at[rows], out_hbm.at[rows], out_sem.at[i]))
+        stores[-1].start()
+    for store in stores:
+        store.wait()
 
 
 def body(
@@ -450,8 +473,8 @@
         + [
             pltpu.VMEM((4, 2 * width, LANES), F32),
             pltpu.VMEM((4, 2 * width, LANES), F32),
-            pltpu.VMEM((devices, 8, LANES), F32),
-            pltpu.VMEM((devices, 8, LANES), F32),
+            pltpu.VMEM((devices, 2 * caps, LANES), F32),
+            pltpu.VMEM((devices, 2 * caps, LANES), F32),
             pltpu.VMEM((devices, 4 * ROWS, LANES), BF16),
             pltpu.VMEM((devices, 2 * ROWS, LANES), BF16),
             sems((len(arrays),)),
@@ -466,17 +489,20 @@
         ),
         name="build_rows",
     )(*arrays)
-    group = 8
+    group = devices // 8
+    full = (devices * capacity, BLOCKS, PAD * PAD)
     return pl.pallas_call(
-        functools.partial(expand_kernel, capacity, count),
-        grid=(devices // group,),
-        out_shape=jax.ShapeDtypeStruct((devices * capacity, BLOCKS, PAD * PAD), BF16),
-        in_specs=[
-            pl.BlockSpec((group, 4 * ROWS, LANES), lambda i: (i, 0, 0)),
-            pl.BlockSpec((group, 2 * ROWS, LANES), lambda i: (i, 0, 0)),
+        functools.partial(expand_kernel, capacity, count, group),
+        out_shape=jax.ShapeDtypeStruct(full, BF16),
+        in_specs=[anywhere] * 2,
+        out_specs=anywhere,
+        scratch_shapes=[
+            pltpu.VMEM(land_off.shape, BF16),
+            pltpu.VMEM(land_diag.shape, BF16),
+            pltpu.VMEM(full, BF16),
+            sems((2, devices // group)),
+            sems((devices // group,)),
         ],
-        out_specs=pl.BlockSpec((group * capacity, BLOCKS, PAD * PAD), lambda i: (i, 0, 0)),
-        scratch_shapes=[pltpu.VMEM((2, group * capacity * BLOCKS, LANES), F32)],
         compiler_params=pltpu.CompilerParams(vmem_limit_bytes=VMEM_LIMIT),
         name="expand_rows",
     )(land_off, land_diag)

time: 34.6 us -> 35.4 us (1.023)
  Pallas kernels: 34.4 us -> 35.2 us
    pallas_call x1, Pallas kernels: 4.29 us -> 4.82 us  [body(): pl.pallas_call(functools.partial(expand_kernel, capacity, count, group),...]
where the time goes in v3:
time: 35.4 us; the launch traced here: 35.2 us
  Pallas kernels  35.2 us (99%)
    pallas_call x1, Pallas kernels, body(): pl.pallas_call(functools.partial(build_kernel, span_x, span_y, width, cou...  30.4 us
    pallas_call x1, Pallas kernels, body(): pl.pallas_call(functools.partial(expand_kernel, capacity, count, group),...  4.82 us

profile of v3, /device:TPU:0, one launch (start us, length us, event | category | flops | bytes accessed | tf_op | source)
XLA Modules:
  0.0 35.2 jit_solution(2247820858202408143)
XLA Ops:
  0.0 30.4 %build_rows.1 = (bf16[32,64,128]{2,1,0:T(8,128)(2,1)}, bf16[32,32,128]{2,1,0:T(8,128)(2,1)}) custom-call(f32[16,16]{1,0:T(8,128)} %bitcast.19, f32[176,16]{1,0:T(8,128)} %bitcast.16, f32[256,121]{1,0:T(8,128)} %bitcast.14, f32[256,121]{1,0:T(8,128)} %bitcast.15, f32[48,16]{1,0:T(8,128)} %bitcast.17, s32[48,16]{1,0:T(8,128)} %bitcast.18, s32[2,32]{1,0:T(2,128)} %bitcast.20, ...), custom_call_target="tpu_custom_call" | custom-call | tf_op jit(solution)/shard_map/build_rows/pallas_call | solution.py:463
  30.4 4.8 %expand_rows.1 = bf16[512,8,256]{2,1,0:T(8,128)(2,1)} custom-call(bf16[32,64,128]{2,1,0:T(8,128)(2,1)} %get-tuple-element.7.off_hbm, bf16[32,32,128]{2,1,0:T(8,128)(2,1)} %get-tuple-element.8.diag_hbm), custom_call_target="tpu_custom_call" | custom-call | tf_op jit(solution)/shard_map/expand_rows/pallas_call | solution.py:494

commit v4 on v2

--- a/solution.py
+++ b/solution.py
@@ -15,7 +15,8 @@
 F32 = jnp.float32
 BF16 = jnp.bfloat16
 NT = (((1,), (1,)), ((), ()))
-VMEM_LIMIT = 60 * 1024 * 1024
+VMEM_LIMIT = 48 * 1024 * 1024
+EXPAND_LIMIT = 32 * 1024 * 1024
 
 
 def iota(shape, dim):
@@ -224,7 +225,7 @@
     index = jnp.where((part & 1) == 0, picks[:, 0:1], picks[:, 1:2])
     hit = iota((lines, cells), 1).astype(F32) == index
     take_l = one_hot(hit & (part < caps))
-    take_m = one_hot(hit & (part >= caps) & (part < 2 * caps))
+    take_m = one_hot(hit & (part >= caps))
     gathered = joined(
         jnp.dot(take_l, jnp.concatenate(split(deriv, 2), 1), preferred_element_type=F32), 2
     ) + joined(
@@ -233,10 +234,6 @@
     fault_out[...] = gathered.reshape(devices, slab, LANES)
     fault_in[pl.ds(me, 1)] = fault_out[pl.ds(me, 1)]
 
-    pl.semaphore_wait(barrier, devices - 1)
-    for side in range(4):
-        pl.when(ends[side])(lambda side=side: halo_copy(side).start())
-    send_all(fault_out, fault_in, 0)
 
     owner = owner_ref[...]
     named = (iota((devices, cells), 0) == owner).astype(F32)
@@ -261,6 +258,11 @@
     where = iota((cells, lines), 1).astype(F32)
     pull_l = one_hot(where == base)
     pull_m = one_hot(where == base + caps)
+
+    pl.semaphore_wait(barrier, devices - 1)
+    for side in range(4):
+        pl.when(ends[side])(lambda side=side: halo_copy(side).start())
+    send_all(fault_out, fault_in, 0)
 
     pressure = misc[:, lane_p : lane_p + 1]
     row = iota((cells, 1), 0)
@@ -370,30 +372,31 @@
     await_all(land_diag, block_rsem.at[2])
 
 
-def expand_kernel(capacity, count, off_ref, diag_ref, out_ref, wide_ref):
-    group = off_ref.shape[0]
+def expand_kernel(capacity, count, group, off_ref, diag_ref, out_ref):
+    kinds = (off_ref.shape[1] + diag_ref.shape[1]) // ROWS
     tall = capacity * BLOCKS
+    kind = iota((tall, kinds * ROWS), 1) // ROWS
+    block = jnp.where(kind < 4, kind + 1, jnp.where(kind == 4, 0, BLOCKS - 1))
+    rank = iota((tall, kinds * ROWS), 1) % ROWS
+    line = iota((tall, kinds * ROWS), 0)
+    order = one_hot((line // BLOCKS == rank) & (line % BLOCKS == block))
     entry = iota((LANES, PAD * PAD), 0)
     target = entry // count * PAD + entry % count
     widen = one_hot((iota((LANES, PAD * PAD), 1) == target) & (entry < count * count))
-    for ref, blocks in ((off_ref, (1, 2, 3, 4)), (diag_ref, (0, BLOCKS - 1))):
-        lines = ref[...].reshape(group * len(blocks) * ROWS, LANES)
-        full = jnp.dot(lines, widen, preferred_element_type=F32)
-        for i in range(group):
-            for j, block in enumerate(blocks):
-                start = (i * len(blocks) + j) * ROWS
-                for half in range(2):
-                    wide_ref[half, pl.ds(i * tall + block, capacity, stride=BLOCKS), :] = full[
-                        start : start + capacity, half * LANES : (half + 1) * LANES
-                    ]
-    gap = jnp.zeros((group * capacity, LANES), F32)
-    for block in (5, 6):
-        for half in range(2):
-            wide_ref[half, pl.ds(block, group * capacity, stride=BLOCKS), :] = gap
-    for half in range(2):
-        out_ref[:, :, half * LANES : (half + 1) * LANES] = (
-            wide_ref[half].astype(BF16).reshape(group * capacity, BLOCKS, LANES)
+    first = pl.program_id(0) * group
+    ordered = []
+    for i in range(0, group, 2):
+        pair = jnp.concatenate(
+            [
+                jnp.concatenate([land[first + i], land[first + i + 1]], 1)
+                for land in (off_ref, diag_ref)
+            ],
+            0,
         )
+        both = jnp.dot(order, pair, preferred_element_type=F32).astype(BF16)
+        ordered += [both[:, :LANES], both[:, LANES:]]
+    full = jnp.dot(jnp.concatenate(ordered, 0), widen, preferred_element_type=F32)
+    out_ref[...] = full.astype(BF16).reshape(group * capacity, BLOCKS, PAD * PAD)
 
 
 def body(
@@ -420,7 +423,7 @@
     caps = fault_send.shape[2]
     assert pressure.shape == (width, width, 1) and caps == 2
     entries = count * count
-    anywhere = pl.BlockSpec(memory_space=pl.ANY)
+    vmem = pl.BlockSpec(memory_space=pltpu.VMEM)
     wide = pltpu.VMEM((cells, LANES), F32)
     sems = pltpu.SemaphoreType.DMA
     arrays = (
@@ -440,18 +443,18 @@
     land_off, land_diag = pl.pallas_call(
         functools.partial(build_kernel, span_x, span_y, width, count),
         out_shape=(
-            jax.ShapeDtypeStruct((devices, 4 * ROWS, LANES), BF16),
-            jax.ShapeDtypeStruct((devices, 2 * ROWS, LANES), BF16),
+            pltpu.VMEM((devices, 4 * ROWS, LANES), BF16),
+            pltpu.VMEM((devices, 2 * ROWS, LANES), BF16),
         ),
         in_specs=[pl.BlockSpec(memory_space=pltpu.HBM)] * 12,
-        out_specs=(anywhere, anywhere),
+        out_specs=(vmem, vmem),
         scratch_shapes=[pltpu.VMEM(array.shape, array.dtype) for array in arrays]
         + [wide] * 6
         + [
             pltpu.VMEM((4, 2 * width, LANES), F32),
             pltpu.VMEM((4, 2 * width, LANES), F32),
-            pltpu.VMEM((devices, 8, LANES), F32),
-            pltpu.VMEM((devices, 8, LANES), F32),
+            pltpu.VMEM((devices, 2 * caps, LANES), F32),
+            pltpu.VMEM((devices, 2 * caps, LANES), F32),
             pltpu.VMEM((devices, 4 * ROWS, LANES), BF16),
             pltpu.VMEM((devices, 2 * ROWS, LANES), BF16),
             sems((len(arrays),)),
@@ -465,19 +468,16 @@
             collective_id=0, has_side_effects=True, vmem_limit_bytes=VMEM_LIMIT
         ),
         name="build_rows",
-    )(*arrays)
-    group = 8
+    )(*[pltpu.with_memory_space_constraint(array, pltpu.HBM) for array in arrays])
+    group = devices // 4
+    full = (devices * capacity, BLOCKS, PAD * PAD)
     return pl.pallas_call(
-        functools.partial(expand_kernel, capacity, count),
+        functools.partial(expand_kernel, capacity, count, group),
         grid=(devices // group,),
-        out_shape=jax.ShapeDtypeStruct((devices * capacity, BLOCKS, PAD * PAD), BF16),
-        in_specs=[
-            pl.BlockSpec((group, 4 * ROWS, LANES), lambda i: (i, 0, 0)),
-            pl.BlockSpec((group, 2 * ROWS, LANES), lambda i: (i, 0, 0)),
-        ],
-        out_specs=pl.BlockSpec((group * capacity, BLOCKS, PAD * PAD), lambda i: (i, 0, 0)),
-        scratch_shapes=[pltpu.VMEM((2, group * capacity * BLOCKS, LANES), F32)],
-        compiler_params=pltpu.CompilerParams(vmem_limit_bytes=VMEM_LIMIT),
+        out_shape=jax.ShapeDtypeStruct(full, BF16),
+        in_specs=[vmem] * 2,
+        out_specs=pl.BlockSpec((group * capacity,) + full[1:], lambda i: (i, 0, 0)),
+        compiler_params=pltpu.CompilerParams(vmem_limit_bytes=EXPAND_LIMIT),
         name="expand_rows",
     )(land_off, land_diag)
 

time: 34.6 us -> 33.3 us (0.962)
  Pallas kernels: 34.4 us -> 33.1 us
    pallas_call x1, Pallas kernels: 4.29 us -> 2.93 us  [body(): pl.pallas_call(functools.partial(expand_kernel, capacity, count, group),...]
where the time goes in v4:
time: 33.3 us; the launch traced here: 33.1 us
  Pallas kernels  33.1 us (99%)
    pallas_call x1, Pallas kernels, body(): pl.pallas_call(functools.partial(build_kernel, span_x, span_y, width, cou...  30.2 us
    pallas_call x1, Pallas kernels, body(): pl.pallas_call(functools.partial(expand_kernel, capacity, count, group),...  2.93 us

profile of v4, /device:TPU:0, one launch (start us, length us, event | category | flops | bytes accessed | tf_op | source)
XLA Modules:
  0.0 33.1 jit_solution(3641619761271687710)
XLA Ops:
  0.0 30.2 %build_rows.1 = (bf16[32,64,128]{2,1,0:T(8,128)(2,1)S(1)}, bf16[32,32,128]{2,1,0:T(8,128)(2,1)S(1)}) custom-call(f32[16,16]{1,0:T(8,128)} %bitcast.19, f32[176,16]{1,0:T(8,128)} %bitcast.16, f32[256,121]{1,0:T(8,128)} %bitcast.14, f32[256,121]{1,0:T(8,128)} %bitcast.15, f32[48,16]{1,0:T(8,128)} %bitcast.17, s32[48,16]{1,0:T(8,128)} %bitcast.18, ...), custom_call_target="tpu_custom_call" | custom-call | tf_op jit(solution)/shard_map/build_rows/pallas_call | solution.py:443
  30.2 2.9 %expand_rows.1 = bf16[512,8,256]{2,1,0:T(8,128)(2,1)} custom-call(bf16[32,64,128]{2,1,0:T(8,128)(2,1)S(1)} %get-tuple-element.7.off_ref, bf16[32,32,128]{2,1,0:T(8,128)(2,1)S(1)} %get-tuple-element.8.diag_ref), custom_call_target="tpu_custom_call" | custom-call | tf_op jit(solution)/shard_map/expand_rows/pallas_call | solution.py:474

commit v5 on v4

--- a/solution.py
+++ b/solution.py
@@ -110,6 +110,9 @@
                 flipped = flipped + (1 - 2 * (ty // (1 << bit) % 2)) * (1 << bit)
         flips.append(flipped)
 
+    half = span_y // 2
+    order = [flip for pair in zip(flips[:half], flips[half:]) for flip in pair]
+
     def each(function):
         def column_of(codes, step):
             x = tx + step
@@ -124,11 +127,8 @@
 
             lax.fori_loop(1, span_x, step_body, 0)
 
-        half = span_y // 2
-        column_of(flips[:half], 0)
-        run(flips[:half])
-        column_of(flips[half : span_y - 1], 0)
-        run(flips[half:])
+        column_of(order[: span_y - 1], 0)
+        run(order)
 
     barrier = pltpu.get_barrier_semaphore()
     each(
@@ -372,31 +372,42 @@
     await_all(land_diag, block_rsem.at[2])
 
 
-def expand_kernel(capacity, count, group, off_ref, diag_ref, out_ref):
+def expand_kernel(capacity, count, group, off_ref, diag_ref, out_hbm, order_ref, widen_ref, out_ref, sem):
     kinds = (off_ref.shape[1] + diag_ref.shape[1]) // ROWS
     tall = capacity * BLOCKS
     kind = iota((tall, kinds * ROWS), 1) // ROWS
     block = jnp.where(kind < 4, kind + 1, jnp.where(kind == 4, 0, BLOCKS - 1))
     rank = iota((tall, kinds * ROWS), 1) % ROWS
     line = iota((tall, kinds * ROWS), 0)
-    order = one_hot((line // BLOCKS == rank) & (line % BLOCKS == block))
+    order_ref[...] = one_hot((line // BLOCKS == rank) & (line % BLOCKS == block))
     entry = iota((LANES, PAD * PAD), 0)
     target = entry // count * PAD + entry % count
-    widen = one_hot((iota((LANES, PAD * PAD), 1) == target) & (entry < count * count))
-    first = pl.program_id(0) * group
-    ordered = []
-    for i in range(0, group, 2):
-        pair = jnp.concatenate(
-            [
-                jnp.concatenate([land[first + i], land[first + i + 1]], 1)
-                for land in (off_ref, diag_ref)
-            ],
-            0,
+    widen_ref[...] = one_hot((iota((LANES, PAD * PAD), 1) == target) & (entry < count * count))
+
+    def piece(step, carry):
+        first = step * group
+        ordered = []
+        for i in range(0, group, 2):
+            pair = jnp.concatenate(
+                [
+                    jnp.concatenate([land[first + i], land[first + i + 1]], 1)
+                    for land in (off_ref, diag_ref)
+                ],
+                0,
+            )
+            both = jnp.dot(order_ref[...], pair, preferred_element_type=F32).astype(BF16)
+            ordered += [both[:, :LANES], both[:, LANES:]]
+        full = jnp.dot(jnp.concatenate(ordered, 0), widen_ref[...], preferred_element_type=F32)
+        out_ref[pl.ds(first * capacity, group * capacity)] = full.astype(BF16).reshape(
+            group * capacity, BLOCKS, PAD * PAD
         )
-        both = jnp.dot(order, pair, preferred_element_type=F32).astype(BF16)
-        ordered += [both[:, :LANES], both[:, LANES:]]
-    full = jnp.dot(jnp.concatenate(ordered, 0), widen, preferred_element_type=F32)
-    out_ref[...] = full.astype(BF16).reshape(group * capacity, BLOCKS, PAD * PAD)
+        for i in range(group):
+            rows = pl.ds((first + i) * capacity, capacity)
+            pltpu.make_async_copy(out_ref.at[rows], out_hbm.at[rows], sem.at[0]).start()
+        return carry
+
+    lax.fori_loop(0, off_ref.shape[0] // group, piece, 0)
+    pltpu.make_async_copy(out_ref, out_hbm, sem.at[0]).wait()
 
 
 def body(
@@ -469,14 +480,19 @@
         ),
         name="build_rows",
     )(*[pltpu.with_memory_space_constraint(array, pltpu.HBM) for array in arrays])
-    group = devices // 4
+    group = devices // 8
     full = (devices * capacity, BLOCKS, PAD * PAD)
     return pl.pallas_call(
         functools.partial(expand_kernel, capacity, count, group),
-        grid=(devices // group,),
         out_shape=jax.ShapeDtypeStruct(full, BF16),
         in_specs=[vmem] * 2,
-        out_specs=pl.BlockSpec((group * capacity,) + full[1:], lambda i: (i, 0, 0)),
+        out_specs=pl.BlockSpec(memory_space=pltpu.HBM),
+        scratch_shapes=[
+            pltpu.VMEM((capacity * BLOCKS, 6 * ROWS), BF16),
+            pltpu.VMEM((LANES, PAD * PAD), BF16),
+            pltpu.VMEM(full, BF16),
+            sems((1,)),
+        ],
         compiler_params=pltpu.CompilerParams(vmem_limit_bytes=EXPAND_LIMIT),
         name="expand_rows",
     )(land_off, land_diag)

time: 33.3 us -> 33.7 us (1.012)
  Pallas kernels: 33.1 us -> 33.5 us
    pallas_call x1, Pallas kernels: 2.93 us -> 3.43 us  [body(): pl.pallas_call(functools.partial(expand_kernel, capacity, count, group),...]
where the time goes in v5:
time: 33.7 us; the launch traced here: 33.5 us
  Pallas kernels  33.5 us (99%)
    pallas_call x1, Pallas kernels, body(): pl.pallas_call(functools.partial(build_kernel, span_x, span_y, width, cou...  30 us
    pallas_call x1, Pallas kernels, body(): pl.pallas_call(functools.partial(expand_kernel, capacity, count, group),...  3.43 us

profile of v5, /device:TPU:0, one launch (start us, length us, event | category | flops | bytes accessed | tf_op | source)
XLA Modules:
  0.0 33.5 jit_solution(15067682621596889385)
XLA Ops:
  0.0 30.0 %build_rows.1 = (bf16[32,64,128]{2,1,0:T(8,128)(2,1)S(1)}, bf16[32,32,128]{2,1,0:T(8,128)(2,1)S(1)}) custom-call(f32[16,16]{1,0:T(8,128)} %bitcast.19, f32[176,16]{1,0:T(8,128)} %bitcast.16, f32[256,121]{1,0:T(8,128)} %bitcast.14, f32[256,121]{1,0:T(8,128)} %bitcast.15, f32[48,16]{1,0:T(8,128)} %bitcast.17, s32[48,16]{1,0:T(8,128)} %bitcast.18, ...), custom_call_target="tpu_custom_call" | custom-call | tf_op jit(solution)/shard_map/build_rows/pallas_call | solution.py:454
  30.1 3.4 %expand_rows.1 = bf16[512,8,256]{2,1,0:T(8,128)(2,1)} custom-call(bf16[32,64,128]{2,1,0:T(8,128)(2,1)S(1)} %get-tuple-element.7.off_ref, bf16[32,32,128]{2,1,0:T(8,128)(2,1)S(1)} %get-tuple-element.8.diag_ref), custom_call_target="tpu_custom_call" | custom-call | tf_op jit(solution)/shard_map/expand_rows/pallas_call | solution.py:485

commit v6 on v4

--- a/solution.py
+++ b/solution.py
@@ -50,8 +50,7 @@
     *refs,
 ):
     sources, refs = refs[:12], refs[12:]
-    land_off, land_diag = refs[:2]
-    inputs, refs = refs[2:14], refs[14:]
+    land, inputs, refs = refs[0], refs[1:13], refs[13:]
     (
         p_ref,
         m_ref,
@@ -77,8 +76,7 @@
         halo_in,
         fault_out,
         fault_in,
-        send_off,
-        send_diag,
+        send,
         input_sem,
         halo_ssem,
         halo_rsem,
@@ -110,25 +108,32 @@
                 flipped = flipped + (1 - 2 * (ty // (1 << bit) % 2)) * (1 << bit)
         flips.append(flipped)
 
+    half = span_y // 2
+    across, near = flips[:half], flips[half:]
+
+    def column_of(function, codes, step):
+        x = tx + step
+        x = x - jnp.where(x >= span_x, span_x, 0)
+        for y in codes:
+            function(x, y)
+
+    def columns_of(function, codes, first):
+        def step_body(step, carry):
+            column_of(function, codes, step)
+            return carry
+
+        lax.fori_loop(first, span_x, step_body, 0)
+
+    def each_across(function):
+        columns_of(function, across, 0)
+
+    def each_near(function):
+        column_of(function, near[:-1], 0)
+        columns_of(function, near, 1)
+
     def each(function):
-        def column_of(codes, step):
-            x = tx + step
-            x = x - jnp.where(x >= span_x, span_x, 0)
-            for y in codes:
-                function(x, y)
-
-        def run(codes):
-            def step_body(step, carry):
-                column_of(codes, step)
-                return carry
-
-            lax.fori_loop(1, span_x, step_body, 0)
-
-        half = span_y // 2
-        column_of(flips[:half], 0)
-        run(flips[:half])
-        column_of(flips[half : span_y - 1], 0)
-        run(flips[half:])
+        each_across(function)
+        each_near(function)
 
     barrier = pltpu.get_barrier_semaphore()
     each(
@@ -137,17 +142,26 @@
         )
     )
 
-    def send_all(src, dst, kind):
-        each(
-            lambda x, y: pltpu.make_async_remote_copy(
-                src_ref=src.at[x * span_y + y],
-                dst_ref=dst.at[me],
-                send_sem=block_ssem.at[kind],
-                recv_sem=block_rsem.at[kind],
-                device_id=(x, y),
-                device_id_type=MESH,
-            ).start()
-        )
+    def row_sender(start, size):
+        lines = pl.ds(start, size)
+        return lambda x, y: pltpu.make_async_remote_copy(
+            src_ref=send.at[x * span_y + y, lines],
+            dst_ref=land.at[me, lines],
+            send_sem=block_ssem.at[1],
+            recv_sem=block_rsem.at[1],
+            device_id=(x, y),
+            device_id_type=MESH,
+        ).start()
+
+    def fault_sender(x, y):
+        pltpu.make_async_remote_copy(
+            src_ref=fault_out.at[x * span_y + y],
+            dst_ref=fault_in.at[me],
+            send_sem=block_ssem.at[0],
+            recv_sem=block_rsem.at[0],
+            device_id=(x, y),
+            device_id_type=MESH,
+        ).start()
 
     def await_all(buffer, sem):
         span = buffer.at[pl.ds(0, devices - 1)]
@@ -262,7 +276,7 @@
     pl.semaphore_wait(barrier, devices - 1)
     for side in range(4):
         pl.when(ends[side])(lambda side=side: halo_copy(side).start())
-    send_all(fault_out, fault_in, 0)
+    each(fault_sender)
 
     pressure = misc[:, lane_p : lane_p + 1]
     row = iota((cells, 1), 0)
@@ -329,19 +343,20 @@
         mobile = mobile + mu
         offs.append(off.astype(BF16))
 
-    def place_rows(parts, buffer):
+    def place_rows(parts, first):
         moved = jnp.dot(
             mover, jnp.concatenate(parts, 1), preferred_element_type=F32
         ).astype(BF16)
         for i in range(len(parts)):
-            buffer[:, i * ROWS : (i + 1) * ROWS, :] = moved[
-                :, i * LANES : (i + 1) * LANES
-            ].reshape(devices, ROWS, LANES)
-
-    place_rows(offs, send_off)
-    send_all(send_off, land_off, 1)
-    own_off = pltpu.make_async_copy(send_off.at[me], land_off.at[me], own_sem.at[0])
-    own_off.start()
+            start = (first + i) * ROWS
+            send[:, start : start + ROWS, :] = moved[:, i * LANES : (i + 1) * LANES].reshape(
+                devices, ROWS, LANES
+            )
+
+    early = 4 * ROWS
+    late = 2 * ROWS
+    place_rows(offs, 0)
+    each_across(row_sender(0, early))
 
     await_all(fault_in, block_rsem.at[0])
     arrived = fault_in[...].reshape(lines, LANES)
@@ -356,24 +371,22 @@
     diag = (scale + part_scale) * deriv + (mobile + mu)
     state_m[...] = diag
     state_m[:, 0:entries] = state_m[:, 0:entries] + acc_ref[...]
-    place_rows([state_m[...].astype(BF16), off.astype(BF16)], send_diag)
-    send_all(send_diag, land_diag, 2)
-    own_diag = pltpu.make_async_copy(send_diag.at[me], land_diag.at[me], own_sem.at[1])
-    own_diag.start()
+    place_rows([state_m[...].astype(BF16), off.astype(BF16)], 4)
+    each_across(row_sender(early, late))
+    each_near(row_sender(0, early + late))
+    own = pltpu.make_async_copy(send.at[me], land.at[me], own_sem.at[0])
+    own.start()
 
     for side in range(4):
         pl.when(ends[side])(lambda side=side: halo_copy(side).wait_send())
     await_all(fault_out, block_ssem.at[0])
-    await_all(send_off, block_ssem.at[1])
-    await_all(send_diag, block_ssem.at[2])
-    own_off.wait()
-    own_diag.wait()
-    await_all(land_off, block_rsem.at[1])
-    await_all(land_diag, block_rsem.at[2])
-
-
-def expand_kernel(capacity, count, group, off_ref, diag_ref, out_ref):
-    kinds = (off_ref.shape[1] + diag_ref.shape[1]) // ROWS
+    await_all(send, block_ssem.at[1])
+    own.wait()
+    await_all(land, block_rsem.at[1])
+
+
+def expand_kernel(capacity, count, group, land, out_ref):
+    kinds = land.shape[1] // ROWS
     tall = capacity * BLOCKS
     kind = iota((tall, kinds * ROWS), 1) // ROWS
     block = jnp.where(kind < 4, kind + 1, jnp.where(kind == 4, 0, BLOCKS - 1))
@@ -386,13 +399,7 @@
     first = pl.program_id(0) * group
     ordered = []
     for i in range(0, group, 2):
-        pair = jnp.concatenate(
-            [
-                jnp.concatenate([land[first + i], land[first + i + 1]], 1)
-                for land in (off_ref, diag_ref)
-            ],
-            0,
-        )
+        pair = jnp.concatenate([land[first + i], land[first + i + 1]], 1)
         both = jnp.dot(order, pair, preferred_element_type=F32).astype(BF16)
         ordered += [both[:, :LANES], both[:, LANES:]]
     full = jnp.dot(jnp.concatenate(ordered, 0), widen, preferred_element_type=F32)
@@ -440,14 +447,11 @@
         fault_up,
         cell_owner.reshape(1, cells),
     )
-    land_off, land_diag = pl.pallas_call(
+    land = pl.pallas_call(
         functools.partial(build_kernel, span_x, span_y, width, count),
-        out_shape=(
-            pltpu.VMEM((devices, 4 * ROWS, LANES), BF16),
-            pltpu.VMEM((devices, 2 * ROWS, LANES), BF16),
-        ),
+        out_shape=pltpu.VMEM((devices, 6 * ROWS, LANES), BF16),
         in_specs=[pl.BlockSpec(memory_space=pltpu.HBM)] * 12,
-        out_specs=(vmem, vmem),
+        out_specs=vmem,
         scratch_shapes=[pltpu.VMEM(array.shape, array.dtype) for array in arrays]
         + [wide] * 6
         + [
@@ -455,14 +459,13 @@
             pltpu.VMEM((4, 2 * width, LANES), F32),
             pltpu.VMEM((devices, 2 * caps, LANES), F32),
             pltpu.VMEM((devices, 2 * caps, LANES), F32),
-            pltpu.VMEM((devices, 4 * ROWS, LANES), BF16),
-            pltpu.VMEM((devices, 2 * ROWS, LANES), BF16),
+            pltpu.VMEM((devices, 6 * ROWS, LANES), BF16),
             sems((len(arrays),)),
             sems((4,)),
             sems((4,)),
-            sems((3,)),
-            sems((3,)),
             sems((2,)),
+            sems((2,)),
+            sems((1,)),
         ],
         compiler_params=pltpu.CompilerParams(
             collective_id=0, has_side_effects=True, vmem_limit_bytes=VMEM_LIMIT
@@ -475,11 +478,11 @@
         functools.partial(expand_kernel, capacity, count, group),
         grid=(devices // group,),
         out_shape=jax.ShapeDtypeStruct(full, BF16),
-        in_specs=[vmem] * 2,
+        in_specs=[vmem],
         out_specs=pl.BlockSpec((group * capacity,) + full[1:], lambda i: (i, 0, 0)),
         compiler_params=pltpu.CompilerParams(vmem_limit_bytes=EXPAND_LIMIT),
         name="expand_rows",
-    )(land_off, land_diag)
+    )(land)
 
 
 def solution(mesh):

time: 33.3 us -> 33.3 us (level)
  no operation moved by 1% of the time
where the time goes in v6:
time: 33.3 us; the launch traced here: 33.1 us
  Pallas kernels  33.1 us (99%)
    pallas_call x1, Pallas kernels, body(): pl.pallas_call(functools.partial(build_kernel, span_x, span_y, width, cou...  30.1 us
    pallas_call x1, Pallas kernels, body(): pl.pallas_call(functools.partial(expand_kernel, capacity, count, group),...  2.96 us

profile of v6, /device:TPU:0, one launch (start us, length us, event | category | flops | bytes accessed | tf_op | source)
XLA Modules:
  0.0 33.1 jit_solution(271531489170005033)
XLA Ops:
  0.0 30.1 %build_rows.1.land = bf16[32,96,128]{2,1,0:T(8,128)(2,1)S(1)} custom-call(f32[16,16]{1,0:T(8,128)} %bitcast.19, f32[176,16]{1,0:T(8,128)} %bitcast.16, f32[256,121]{1,0:T(8,128)} %bitcast.14, f32[256,121]{1,0:T(8,128)} %bitcast.15, f32[48,16]{1,0:T(8,128)} %bitcast.17, s32[48,16]{1,0:T(8,128)} %bitcast.18, s32[2,32]{1,0:T(2,128)} %bitcast.20, ...), custom_call_target="tpu_custom_call" | custom-call | tf_op jit(solution)/shard_map/build_rows/pallas_call | solution.py:450
  30.1 3.0 %expand_rows.1 = bf16[512,8,256]{2,1,0:T(8,128)(2,1)} custom-call(bf16[32,96,128]{2,1,0:T(8,128)(2,1)S(1)} %build_rows.1.land), custom_call_target="tpu_custom_call" | custom-call | tf_op jit(solution)/shard_map/expand_rows/pallas_call | solution.py:477

commit v7 on v6

--- a/solution.py
+++ b/solution.py
@@ -68,10 +68,11 @@
     (
         state_l,
         state_m,
-        lower_y_l,
-        lower_y_m,
-        upper_y_l,
-        upper_y_m,
+        near_l,
+        near_m,
+        rates,
+        offs,
+        total,
         halo_out,
         halo_in,
         fault_out,
@@ -273,23 +274,62 @@
     pull_l = one_hot(where == base)
     pull_m = one_hot(where == base + caps)
 
+    row = iota((cells, 1), 0)
+    at_x = row >> shift
+    at_y = row & (width - 1)
+
+    def column(array, lane):
+        return array[:, lane : lane + 1]
+
+    def terms(own_l, own_m, other_l, other_m, conduct, flag):
+        lower = 1.0 - flag
+        diff = column(own_m, lane_p) - column(other_m, lane_p)
+        mu = (conduct * flag) * own_m + (conduct * lower) * other_m
+        off = (conduct * lower * diff) * other_l - mu
+        return (conduct * flag * diff) * own_l + mu, off
+
+    for kept, field in ((near_l, deriv), (near_m, misc)):
+        kept[0, width:] = field[:last]
+        kept[0, 0:width] = jnp.zeros((width, LANES), F32)
+        kept[1, 0:last] = field[width:]
+        kept[1, last:] = jnp.zeros((width, LANES), F32)
+        kept[2] = pltpu.roll(field, 1, 0)
+        kept[3] = pltpu.roll(field, cells - 1, 0)
+    inside = (at_x > 0, at_x < width - 1, at_y > 0, at_y < width - 1)
+    for side in range(4):
+        axis = side // 2
+        if side % 2:
+            conduct, flag = column(misc, lane_t + axis), column(misc, lane_w + axis)
+        else:
+            lower_m = near_m[side]
+            conduct = column(lower_m, lane_t + axis)
+            flag = 1.0 - column(lower_m, lane_w + axis)
+        rates[side, :, 0:1] = jnp.where(inside[side], conduct, 0.0)
+        rates[side, :, 1:2] = flag
+    total[...] = jnp.zeros_like(total)
+    total[:, 0:entries] = acc_ref[...]
+
+    def inner(side, carry):
+        rate = rates[side]
+        added, off = terms(
+            state_l[...],
+            state_m[...],
+            near_l[side],
+            near_m[side],
+            column(rate, 0),
+            column(rate, 1),
+        )
+        total[...] += added
+        offs[side] = off
+        return carry
+
+    lax.fori_loop(0, 4, inner, 0)
+
     pl.semaphore_wait(barrier, devices - 1)
     for side in range(4):
         pl.when(ends[side])(lambda side=side: halo_copy(side).start())
     each(fault_sender)
 
-    pressure = misc[:, lane_p : lane_p + 1]
-    row = iota((cells, 1), 0)
-    at_x = row >> shift
-    at_y = row & (width - 1)
-
-    def terms(other_l, other_m, conduct, flag):
-        lower = 1.0 - flag
-        diff = pressure - other_m[:, lane_p : lane_p + 1]
-        mu = (conduct * flag) * misc + (conduct * lower) * other_m
-        off = (conduct * lower * diff) * other_l - mu
-        return conduct * flag * diff, mu, off
-
     for side in range(4):
         @pl.when(ends[side])
         def _(side=side):
@@ -299,49 +339,27 @@
         def _(side=side):
             halo_in[side] = jnp.zeros_like(halo_in[side])
 
-    def column(array, lane):
-        return array[:, lane : lane + 1]
-
-    near_l = jnp.concatenate([halo_in[0, 0:width], deriv[:last]], 0)
-    near_m = jnp.concatenate([halo_in[0, width : 2 * width], misc[:last]], 0)
-    far_l = jnp.concatenate([deriv[width:], halo_in[1, 0:width]], 0)
-    far_m = jnp.concatenate([misc[width:], halo_in[1, width : 2 * width]], 0)
-    for kept, field, rows, amount, start, side in (
-        (lower_y_l, deriv, slice(0, width), 1, 0, 2),
-        (lower_y_m, misc, slice(width, 2 * width), 1, 0, 2),
-        (upper_y_l, deriv, slice(0, width), cells - 1, width - 1, 3),
-        (upper_y_m, misc, slice(width, 2 * width), cells - 1, width - 1, 3),
+    for side, rows in enumerate(
+        (
+            pl.ds(0, width),
+            pl.ds(last, width),
+            pl.ds(0, width, stride=width),
+            pl.ds(width - 1, width, stride=width),
+        )
     ):
-        kept[...] = pltpu.roll(field, amount, 0)
-        kept[pl.ds(start, width, stride=width), :] = halo_in[side, rows, :]
-
-    keep_x = jnp.where((at_x < width - 1) | (tx < span_x - 1), 1.0, 0.0)
-    keep_y = jnp.where((at_y < width - 1) | (ty < span_y - 1), 1.0, 0.0)
-    low_y_m = lower_y_m[...]
-    sides = (
-        (near_l, near_m, column(near_m, lane_t), 1.0 - column(near_m, lane_w)),
-        (far_l, far_m, column(misc, lane_t) * keep_x, column(misc, lane_w)),
-        (
-            lower_y_l[...],
-            low_y_m,
-            column(low_y_m, lane_t + 1),
-            1.0 - column(low_y_m, lane_w + 1),
-        ),
-        (
-            upper_y_l[...],
-            upper_y_m[...],
-            column(misc, lane_t + 1) * keep_y,
-            column(misc, lane_w + 1),
-        ),
-    )
-    scale = jnp.zeros((cells, 1), F32)
-    mobile = jnp.zeros((cells, LANES), F32)
-    offs = []
-    for other_l, other_m, conduct, flag in sides:
-        part_scale, mu, off = terms(other_l, other_m, conduct, flag)
-        scale = scale + part_scale
-        mobile = mobile + mu
-        offs.append(off.astype(BF16))
+        axis = side // 2
+        own_l, own_m = state_l[rows, :], state_m[rows, :]
+        other_l = halo_in[side, 0:width]
+        other_m = halo_in[side, width : 2 * width]
+        if side % 2:
+            conduct = column(own_m, lane_t + axis) * jnp.where(ends[side], 1.0, 0.0)
+            flag = column(own_m, lane_w + axis)
+        else:
+            conduct = column(other_m, lane_t + axis)
+            flag = 1.0 - column(other_m, lane_w + axis)
+        added, off = terms(own_l, own_m, other_l, other_m, conduct, flag)
+        total[rows, :] = total[rows, :] + added
+        offs[side, rows, :] = off
 
     def place_rows(parts, first):
         moved = jnp.dot(
@@ -355,7 +373,7 @@
 
     early = 4 * ROWS
     late = 2 * ROWS
-    place_rows(offs, 0)
+    place_rows([offs[side].astype(BF16) for side in range(4)], 0)
     each_across(row_sender(0, early))
 
     await_all(fault_in, block_rsem.at[0])
@@ -367,11 +385,10 @@
     other_m = joined(
         jnp.dot(pull_m, jnp.concatenate(pieces, 1), preferred_element_type=F32), 3
     )
-    part_scale, mu, off = terms(other_l, other_m, fault_conduct, fault_flag)
-    diag = (scale + part_scale) * deriv + (mobile + mu)
-    state_m[...] = diag
-    state_m[:, 0:entries] = state_m[:, 0:entries] + acc_ref[...]
-    place_rows([state_m[...].astype(BF16), off.astype(BF16)], 4)
+    added, off = terms(
+        state_l[...], state_m[...], other_l, other_m, fault_conduct, fault_flag
+    )
+    place_rows([(total[...] + added).astype(BF16), off.astype(BF16)], 4)
     each_across(row_sender(early, late))
     each_near(row_sender(0, early + late))
     own = pltpu.make_async_copy(send.at[me], land.at[me], own_sem.at[0])
@@ -453,7 +470,9 @@
         in_specs=[pl.BlockSpec(memory_space=pltpu.HBM)] * 12,
         out_specs=vmem,
         scratch_shapes=[pltpu.VMEM(array.shape, array.dtype) for array in arrays]
-        + [wide] * 6
+        + [wide] * 2
+        + [pltpu.VMEM((4, cells, LANES), F32)] * 4
+        + [wide]
         + [
             pltpu.VMEM((4, 2 * width, LANES), F32),
             pltpu.VMEM((4, 2 * width, LANES), F32),

time: 33.3 us -> 33.3 us (level)
  no operation moved by 1% of the time
where the time goes in v7:
time: 33.3 us; the launch traced here: 33.1 us
  Pallas kernels  33.1 us (99%)
    pallas_call x1, Pallas kernels, body(): pl.pallas_call(functools.partial(build_kernel, span_x, span_y, width, cou...  30.1 us
    pallas_call x1, Pallas kernels, body(): pl.pallas_call(functools.partial(expand_kernel, capacity, count, group),...  2.96 us

profile of v7, /device:TPU:0, one launch (start us, length us, event | category | flops | bytes accessed | tf_op | source)
XLA Modules:
  0.0 33.1 jit_solution(12789128272856062743)
XLA Ops:
  0.0 30.1 %build_rows.1.land = bf16[32,96,128]{2,1,0:T(8,128)(2,1)S(1)} custom-call(f32[16,16]{1,0:T(8,128)} %bitcast.19, f32[176,16]{1,0:T(8,128)} %bitcast.16, f32[256,121]{1,0:T(8,128)} %bitcast.14, f32[256,121]{1,0:T(8,128)} %bitcast.15, f32[48,16]{1,0:T(8,128)} %bitcast.17, s32[48,16]{1,0:T(8,128)} %bitcast.18, s32[2,32]{1,0:T(2,128)} %bitcast.20, ...), custom_call_target="tpu_custom_call" | custom-call | tf_op jit(solution)/shard_map/build_rows/pallas_call | solution.py:467
  30.1 3.0 %expand_rows.1 = bf16[512,8,256]{2,1,0:T(8,128)(2,1)} custom-call(bf16[32,96,128]{2,1,0:T(8,128)(2,1)S(1)} %build_rows.1.land), custom_call_target="tpu_custom_call" | custom-call | tf_op jit(solution)/shard_map/expand_rows/pallas_call | solution.py:496

commit v8 on v7

--- a/solution.py
+++ b/solution.py
@@ -323,12 +323,11 @@
         offs[side] = off
         return carry
 
-    lax.fori_loop(0, 4, inner, 0)
-
     pl.semaphore_wait(barrier, devices - 1)
     for side in range(4):
         pl.when(ends[side])(lambda side=side: halo_copy(side).start())
     each(fault_sender)
+    lax.fori_loop(0, 4, inner, 0)
 
     for side in range(4):
         @pl.when(ends[side])
@@ -420,7 +419,7 @@
         both = jnp.dot(order, pair, preferred_element_type=F32).astype(BF16)
         ordered += [both[:, :LANES], both[:, LANES:]]
     full = jnp.dot(jnp.concatenate(ordered, 0), widen, preferred_element_type=F32)
-    out_ref[...] = full.astype(BF16).reshape(group * capacity, BLOCKS, PAD * PAD)
+    out_ref[...] = full.reshape(group * capacity, BLOCKS, PAD * PAD).astype(BF16)
 
 
 def body(

time: 33.3 us -> 32.6 us (0.979)
  Pallas kernels: 33.1 us -> 32.4 us
    pallas_call x1, Pallas kernels: 30.1 us -> 29.4 us  [body(): pl.pallas_call(functools.partial(build_kernel, span_x, span_y, width, cou...]
where the time goes in v8:
time: 32.6 us; the launch traced here: 32.4 us
  Pallas kernels  32.4 us (99%)
    pallas_call x1, Pallas kernels, body(): pl.pallas_call(functools.partial(build_kernel, span_x, span_y, width, cou...  29.4 us
    pallas_call x1, Pallas kernels, body(): pl.pallas_call(functools.partial(expand_kernel, capacity, count, group),...  2.97 us

profile of v8, /device:TPU:0, one launch (start us, length us, event | category | flops | bytes accessed | tf_op | source)
XLA Modules:
  0.0 32.4 jit_solution(13067432945747714697)
XLA Ops:
  0.0 29.4 %build_rows.1.land = bf16[32,96,128]{2,1,0:T(8,128)(2,1)S(1)} custom-call(f32[16,16]{1,0:T(8,128)} %bitcast.19, f32[176,16]{1,0:T(8,128)} %bitcast.16, f32[256,121]{1,0:T(8,128)} %bitcast.14, f32[256,121]{1,0:T(8,128)} %bitcast.15, f32[48,16]{1,0:T(8,128)} %bitcast.17, s32[48,16]{1,0:T(8,128)} %bitcast.18, s32[2,32]{1,0:T(2,128)} %bitcast.20, ...), custom_call_target="tpu_custom_call" | custom-call | tf_op jit(solution)/shard_map/build_rows/pallas_call | solution.py:466
  29.4 3.0 %expand_rows.1 = bf16[512,8,256]{2,1,0:T(8,128)(2,1)} custom-call(bf16[32,96,128]{2,1,0:T(8,128)(2,1)S(1)} %build_rows.1.land), custom_call_target="tpu_custom_call" | custom-call | tf_op jit(solution)/shard_map/expand_rows/pallas_call | solution.py:495
